TPU v7x, 1024 devices: a whole 8x8x8 slice. The times are simulated.
1024 devices in a mesh: dp: 32 (over y_hi, x, core), expert: 32 (over z, y_lo).
Axes of the slice: x: 8, y: 8 (y_hi: 2, y_lo: 4; y = y_hi * 4 + y_lo), z: 8, core: 2. Of those that a mesh axis runs over, the one named last changes fastest.
Arguments:
- grads: bfloat16 [32, 288, 57344], P('dp', 'expert'), may hold values from -6 to 6
- weights: bfloat16 [256, 57344], P('expert', 'dp'), may hold values from -3 to 3
- first: float32 [256, 57344], P('expert', 'dp'), may hold values from -3 to 3
- second: float32 [256, 57344], P('expert', 'dp'), may hold values from 0.25 to 1
- old_home: int32 [256], replicated, may hold values from 0 to 255, as said below
- old_extra: int32 [32], replicated, may hold values from 0 to 255, as said below
- new_home: int32 [256], replicated, may hold values from 0 to 255, as said below
- new_extra: int32 [32], replicated, may hold values from 0 to 255, as said below
Outputs:
- new_weights: bfloat16 [288, 57344], P('expert', 'dp')
- new_first: float32 [256, 57344], P('expert', 'dp')
- new_second: float32 [256, 57344], P('expert', 'dp')
Inputs may be any that keep to these rules, and one draw needn't show every extreme that they name: `old_home`: A permutation of the expert ids. `new_home`: A permutation of the expert ids. Exactly one home slot of each expert device holds under new_home an expert whose old home slot lies on another expert device; the other home slots keep their experts. `old_extra`: expert ids; an expert may fill several redundant slots. `new_extra`: expert ids; an expert may fill several redundant slots.
All inputs are finite; a program needn't handle non-finite values.
Results may differ from a plain program's by a relative error of at most 0.0004.
Values may be sent and summed in bfloat16 or wider, within the bound.
No kernel may reach another device: no remote copies, remote signals or barrier semaphores. Data moves between devices by JAX's collectives and lax.ppermute only.
A program may use at most 32 MiB of HBM per device.

v0:
```python
import jax
import jax.numpy as jnp
from jax import lax
from jax.sharding import PartitionSpec as P

bias_first = 0.9999734386011124
bias_second = 0.994079470779696


def place_of(wanted, table):
    positions = jnp.arange(table.shape[0], dtype=jnp.int32)
    return jnp.sum(jnp.where(wanted[:, None] == table[None, :], positions[None, :], 0), axis=1)


def per_device(grads, weights, first, second, old_home, old_extra, new_home, new_extra):
    homes = weights.shape[0]
    extras = grads.shape[1] - homes
    highest = lax.Precision.HIGHEST
    summed = lax.psum_scatter(grads[0].astype(jnp.float32), "dp", scatter_dimension=1, tiled=True)
    me = lax.axis_index("expert")
    devices = lax.axis_size("expert")
    extra_grads = lax.all_gather(summed[homes:], "expert", axis=0, tiled=True)
    my_home = lax.dynamic_slice_in_dim(old_home, me * homes, homes)
    match = (my_home[:, None] == old_extra[None, :]).astype(jnp.float32)
    total = summed[:homes] + jnp.dot(match, extra_grads, precision=highest)
    moment1 = 0.9 * first + 0.1 * total
    moment2 = 0.95 * second + 0.05 * total * total
    base = weights.astype(jnp.float32)
    step = moment1 / bias_first / (jnp.sqrt(moment2 / bias_second) + 1e-08)
    updated = (base - 0.02 * (step + 0.1 * base)).astype(jnp.bfloat16)
    updated_wide = updated.astype(jnp.float32)
    new_place = place_of(old_home, new_home)
    slot_ids = jnp.arange(old_home.shape[0], dtype=jnp.int32)
    leaving = (new_place // homes != slot_ids // homes).astype(jnp.int32).reshape(devices, homes)
    picked = jnp.argmax(leaving, axis=1)
    sent_place = jnp.arange(devices, dtype=jnp.int32) * homes + picked
    mine = lax.dynamic_index_in_dim(picked, me, 0, keepdims=True)
    outgoing = (
        lax.dynamic_slice_in_dim(updated_wide, mine[0], 1),
        lax.dynamic_slice_in_dim(moment1, mine[0], 1),
        lax.dynamic_slice_in_dim(moment2, mine[0], 1),
    )
    arrived_w, arrived_m, arrived_v = (
        lax.all_gather(outgoing[0], "expert", axis=0, tiled=True),
        lax.all_gather(outgoing[1], "expert", axis=0, tiled=True),
        lax.all_gather(outgoing[2], "expert", axis=0, tiled=True),
    )
    need = lax.dynamic_slice_in_dim(new_home, me * homes, homes)
    source = place_of(need, old_home)
    local_ids = me * homes + jnp.arange(homes, dtype=jnp.int32)
    local_pick = (source[:, None] == local_ids[None, :]).astype(jnp.float32)
    remote_pick = (
        (source[:, None] == sent_place[None, :]) & (source // homes != me)[:, None]
    ).astype(jnp.float32)
    new_first = jnp.dot(local_pick, moment1, precision=highest) + jnp.dot(
        remote_pick, arrived_m, precision=highest
    )
    new_second = jnp.dot(local_pick, moment2, precision=highest) + jnp.dot(
        remote_pick, arrived_v, precision=highest
    )
    home_weights = (
        jnp.dot(local_pick, updated_wide, precision=highest)
        + jnp.dot(remote_pick, arrived_w, precision=highest)
    ).astype(jnp.bfloat16)
    wanted = lax.dynamic_slice_in_dim(new_extra, me * extras, extras)
    wanted_place = place_of(wanted, old_home)
    piece = lax.all_gather(updated, "expert", axis=0, tiled=True)
    count = piece.shape[0]
    select = (wanted_place[:, None] == jnp.arange(count, dtype=jnp.int32)[None, :]).astype(
        jnp.float32
    )
    extra_weights = jnp.dot(select, piece.astype(jnp.float32), precision=highest).astype(
        jnp.bfloat16
    )
    new_weights = jnp.concatenate([home_weights, extra_weights], axis=0)
    return (new_weights, new_first, new_second)


def solution(mesh):
    placed = (
        P("dp", "expert", None),
        P("expert", "dp"),
        P("expert", "dp"),
        P("expert", "dp"),
        P(),
        P(),
        P(),
        P(),
    )
    return jax.shard_map(
        per_device,
        mesh=mesh,
        in_specs=placed,
        out_specs=(P("expert", "dp"), P("expert", "dp"), P("expert", "dp")),
        check_vma=False,
    )
```

profile of v0, /device:TPU:14, one launch (start us, length us, event | category | flops | bytes accessed | tf_op | source)
XLA Modules:
  0.0 581.1 jit_solution(14305169075204375472)
XLA Ops:
  7.2 0.0 copy-start.3
  7.2 0.0 copy-start.4
  7.2 0.0 copy-start.6
  7.2 0.0 copy-start.2
  7.2 0.0 copy-start
  7.2 0.0 copy-start.1
  7.2 0.0 copy-start.5
  7.2 0.0 reduce-scatter.2.cloned.1.call-start
  7.3 3.5 bitcast_convert_fusion
  10.8 0.0 reduce-scatter.2.cloned.1.call-update
  10.9 0.0 copy-done.3
  10.9 0.1 dynamic_slice.23
  10.9 0.0 copy-done.4
  11.0 0.1 dynamic_slice.22
  11.0 0.2 select_reduce_fusion
  11.2 0.1 reduce_sum.31
  11.3 0.7 iota_reduce_fusion
  12.0 0.6 dynamic_slice.24
  13.8 0.0 copy-done.6
  13.8 0.6 dynamic_slice.26
  14.4 1.3 fusion.44
  15.7 0.6 iota_compare_fusion
  17.0 0.2 select_reduce_fusion.1
  17.2 161.7 %reduce-scatter.2.cloned.1.call-done = f32[9,1792]{1,0:T(8,128)} async-done(((f32[9,57344]{1,0:T(8,128)}), f32[9,1792]{1,0:T(8,128)}) %reduce-scatter.2.cloned.1.call-update) | async-done | bytes 64528 | tf_op jit(solution)/shard_map/reduce_scatter | solution.py:19
  178.9 0.8 slice_bitcast_fusion
  179.7 80.9 %all-gather = f32[32,1,1792]{2,1,0:T(1,128)S(1)} all-gather(f32[1,1,1792]{2,1,0:T(1,128)S(1)} %slice_bitcast_fusion), channel_id=1, replica_groups=mesh['dp'=32,'expert'=32] {'expert'}, dimensions={0}, use_global_device_ids=true | all-gather | bytes 236544 | tf_op jit(solution)/shard_map/all_gather | solution.py:22
  260.6 0.0 copy-done.2
  260.6 0.0 copy-done
  260.6 0.0 copy-done.1
  260.6 0.0 copy-done.5
  260.6 1.1 fusion.11
  261.7 81.2 %all_gather.17 = bf16[256,1792]{1,0:T(8,128)(2,1)S(1)} all-gather(bf16[8,1792]{1,0:T(8,128)(2,1)S(1)} %get-tuple-element.5), channel_id=1, replica_groups=mesh['dp'=32,'expert'=32] {'expert'}, dimensions={0}, use_global_device_ids=true | all-gather | bytes 946176 | tf_op jit(solution)/shard_map/all_gather | solution.py:67
  342.9 0.2 fusion.24
  343.1 0.2 fusion.22
  343.4 0.2 fusion.20
  343.6 0.3 convolution_reduce_fusion
  343.9 76.7 %all-gather.1 = f32[32,1,1792]{2,1,0:T(1,128)S(1)} all-gather(f32[1,1,1792]{2,1,0:T(1,128)S(1)} %fusion.19), channel_id=1, replica_groups=mesh['dp'=32,'expert'=32] {'expert'}, dimensions={0}, use_global_device_ids=true | all-gather | bytes 236544 | tf_op jit(solution)/shard_map/all_gather | solution.py:44
  420.6 74.7 %all-gather.2 = f32[32,1,1792]{2,1,0:T(1,128)S(1)} all-gather(f32[1,1,1792]{2,1,0:T(1,128)S(1)} %dynamic-slice_bitcast_fusion.1), channel_id=1, replica_groups=mesh['dp'=32,'expert'=32] {'expert'}, dimensions={0}, use_global_device_ids=true | all-gather | bytes 236544 | tf_op jit(solution)/shard_map/all_gather | solution.py:45
  495.3 76.4 %all-gather.3 = f32[32,1,1792]{2,1,0:T(1,128)S(1)} all-gather(f32[1,1,1792]{2,1,0:T(1,128)S(1)} %dynamic-slice_bitcast_fusion), channel_id=1, replica_groups=mesh['dp'=32,'expert'=32] {'expert'}, dimensions={0}, use_global_device_ids=true | all-gather | bytes 236544 | tf_op jit(solution)/shard_map/all_gather | solution.py:46
  571.7 0.2 fusion
  571.9 0.6 pad_maximum_fusion
  572.6 0.9 convolution_add_fusion.1
  573.4 0.9 convolution_add_fusion
  (8 shorter events, 0.1 us)
Async XLA Ops:
  7.2 3.7 copy-start.3
  7.2 3.8 copy-start.4
  7.2 6.7 %copy-start.6 = (s32[32]{0:T(128)S(1)}, s32[32]{0:T(128)}, u32[]{:S(2)}) copy-start(s32[32]{0:T(128)} %param.15) | copy-start | bytes 388
  7.2 253.4 %copy-start.2 = (bf16[8,1792]{1,0:T(8,128)(2,1)S(1)}, bf16[8,1792]{1,0:T(8,128)(2,1)}, u32[]{:S(2)}) copy-start(bf16[8,1792]{1,0:T(8,128)(2,1)} %param.9) | copy-start | bytes 86020
  7.2 253.4 %copy-start = (f32[8,1792]{1,0:T(8,128)S(1)}, f32[8,1792]{1,0:T(8,128)}, u32[]{:S(2)}) copy-start(f32[8,1792]{1,0:T(8,128)} %param.10) | copy-start | bytes 172036
  7.2 253.4 %copy-start.1 = (f32[8,1792]{1,0:T(8,128)S(1)}, f32[8,1792]{1,0:T(8,128)}, u32[]{:S(2)}) copy-start(f32[8,1792]{1,0:T(8,128)} %param.11) | copy-start | bytes 172036
  7.2 253.4 %copy-start.5 = (s32[32]{0:T(128)S(1)}, s32[32]{0:T(128)}, u32[]{:S(2)}) copy-start(s32[32]{0:T(128)} %param.13) | copy-start | bytes 388
  7.2 171.7 %reduce-scatter.2.cloned.1.call-start = ((), (), s32[]{:S(2)}) async-start(), calls=%async_computation.1 | async-start | bytes 3784704 | tf_op jit(solution)/shard_map/reduce_scatter | solution.py:19
Sparse Core Ops, SparseCore 0:
  14.0 164.8 reduce-scatter.1
where the time goes:
time: 582 us; the launch traced here: 581 us
  blocking collectives  390 us (67%)
  waiting for transfers between devices  162 us (28%)
  between operations  16.2 us (3%)
  other arithmetic  7.17 us (1%)
    reduce_scatter x1, waiting for transfers between devices, per_device(): lax.psum_scatter(grads[0].astype(jnp.float32), 'dp', scatter_dimension=1,...  162 us
    all_gather x1, blocking collectives, per_device(): piece = lax.all_gather(updated, 'expert', axis=0, tiled=True)  81.2 us
    all_gather x1, blocking collectives, per_device(): extra_grads = lax.all_gather(summed[homes:], 'expert', axis=0, tiled=True)  80.9 us
    all_gather x1, blocking collectives, per_device(): lax.all_gather(outgoing[0], 'expert', axis=0, tiled=True)  76.7 us
    all_gather x1, blocking collectives, per_device(): lax.all_gather(outgoing[2], 'expert', axis=0, tiled=True)  76.4 us
    all_gather x1, blocking collectives, per_device(): lax.all_gather(outgoing[1], 'expert', axis=0, tiled=True)  74.7 us
  transfers between devices with their start and end apart: 1, of which 1 were waited for; matrix products, arithmetic and copies ran while one was open for 1% of the time, Pallas kernels for 0%

commit v1 on v0

v1 whole, which is shorter than its diff:
```python
import jax
import jax.numpy as jnp
from jax import lax
from jax.experimental import pallas as pl
from jax.experimental.pallas import tpu as pltpu
from jax.sharding import Mesh
from jax.sharding import PartitionSpec as P

bias_first = 0.9999734386011124
bias_second = 0.994079470779696
LANES = 128
ROW = 16
PAIR_SCALE = 4096.0
SUM_SCALE = 256.0
STATE_SCALE = 16384.0

F32 = jnp.float32
F16 = jnp.float16
BF16 = jnp.bfloat16
VMEM = pl.BlockSpec(memory_space=pltpu.VMEM)
SMEM = pl.BlockSpec(memory_space=pltpu.SMEM)


def cost(n):
    return pl.CostEstimate(flops=n, bytes_accessed=4 * n, transcendentals=0)


def split_kernel(homes, width, steps, grads_ref, out_ref, line):
    tiles = width // LANES
    line[...] = jnp.zeros_like(line)
    for j in range(steps):
        for c in range(2):
            at = (2 * j + c) * width
            block = grads_ref[0, :, at : at + width].astype(F32)
            for t in range(0, tiles, 2):
                low = block[:homes, t * LANES : (t + 1) * LANES]
                high = block[:homes, (t + 1) * LANES : (t + 2) * LANES]
                out_ref[c, j, t * homes : (t + 2) * homes, :] = jnp.concatenate([low, high], axis=0).astype(BF16)
            for t in range(tiles):
                line[t : t + 1, :] = block[homes : homes + 1, t * LANES : (t + 1) * LANES]
            out_ref[c, j, tiles * homes : tiles * homes + ROW, :] = line[...].astype(BF16)


def split_by_core(grads, outer, width):
    homes = grads.shape[1] - 1
    rows = (width // LANES) * homes + ROW
    steps = 4 if outer % 4 == 0 else 1
    return pl.pallas_call(
        lambda *refs: split_kernel(homes, width, steps, *refs),
        grid=(outer // steps,),
        in_specs=[pl.BlockSpec((1, homes + 1, steps * 2 * width), lambda i: (0, 0, i))],
        out_specs=pl.BlockSpec((2, steps, rows, LANES), lambda i: (0, i, 0, 0)),
        out_shape=jax.ShapeDtypeStruct((2, outer, rows, LANES), BF16),
        scratch_shapes=[pltpu.VMEM((ROW, LANES), F32)],
        compiler_params=pltpu.CompilerParams(vmem_limit_bytes=16 * 2**20),
        cost_estimate=cost(1 << 19),
    )(grads)


def state_kernel(scal, w_ref, f_ref, s_ref, out_ref, rows):
    homes, width = f_ref.shape
    tiles = width // LANES
    rows[...] = jnp.zeros_like(rows)
    for n, ref in enumerate((w_ref, f_ref, s_ref)):
        value = ref[...].astype(F32) * STATE_SCALE
        for i in range(homes):
            for t in range(tiles):
                rows[i, n * ROW + t : n * ROW + t + 1, :] = value[i : i + 1, t * LANES : (t + 1) * LANES]
    leaving = rows[scal[0]]
    for d in range(out_ref.shape[0]):
        out_ref[d, : 3 * ROW, :] = leaving
        out_ref[d, 3 * ROW :, :] = rows[scal[8 + d]]


def sums_kernel(scal, s_ref, out_ref, rows):
    homes = rows.shape[0]
    tiles = (s_ref.shape[0] - ROW) // homes
    rows[...] = jnp.zeros_like(rows)
    for i in range(homes):
        for t in range(tiles):
            rows[i, t : t + 1, :] = s_ref[t * homes + i : t * homes + i + 1, :]
    extra = s_ref[tiles * homes :, :]
    leaving = rows[scal[0]]
    for d in range(out_ref.shape[0]):
        out_ref[d, :ROW, :] = extra
        out_ref[d, ROW : 2 * ROW, :] = leaving
        out_ref[d, 2 * ROW :, :] = rows[scal[8 + d]]


def adam(total, base, first, second):
    moment1 = 0.9 * first + 0.1 * total
    moment2 = 0.95 * second + 0.05 * total * total
    step = moment1 / bias_first / (jnp.sqrt(moment2 / bias_second) + 1e-08)
    return base - 0.02 * (step + 0.1 * base), moment1, moment2


def final_kernel(scal, sums_ref, late_ref, early_ref, w_ref, f_ref, s_ref, nw_ref, nf_ref, ns_ref, acc, flat):
    homes, width = f_ref.shape
    tiles = width // LANES
    devices = late_ref.shape[0]
    slot = scal[0]
    acc[...] = jnp.zeros_like(acc)
    acc[slot] = late_ref[scal[1], ROW : 2 * ROW, :]
    acc[homes] = late_ref[scal[2], 2 * ROW :, :]
    for s in range(devices):
        to = scal[8 + devices + s]

        @pl.when(to >= 0)
        def _():
            acc[to] += late_ref[s, :ROW, :]

        @pl.when(scal[8 + 2 * devices + s] > 0)
        def _():
            acc[homes] += late_ref[s, :ROW, :]

    for t in range(tiles):
        for i in range(homes + 1):
            flat[i : i + 1, t * LANES : (t + 1) * LANES] = acc[i, t : t + 1, :]
    is_new = lax.broadcasted_iota(jnp.int32, (homes, LANES), 0) == slot
    for t in range(tiles):
        cols = slice(t * LANES, (t + 1) * LANES)
        total = flat[:homes, cols] + jnp.where(is_new, 0.0, sums_ref[t * homes : (t + 1) * homes, :])
        base = jnp.where(is_new, early_ref[0:1, cols], w_ref[:, cols].astype(F32))
        first = jnp.where(is_new, early_ref[1:2, cols], f_ref[:, cols])
        second = jnp.where(is_new, early_ref[2:3, cols], s_ref[:, cols])
        updated, moment1, moment2 = adam(total, base, first, second)
        extra, _, _ = adam(flat[homes : homes + 1, cols], early_ref[3:4, cols], early_ref[4:5, cols], early_ref[5:6, cols])
        nf_ref[:, cols] = moment1
        ns_ref[:, cols] = moment2
        nw_ref[:, cols] = jnp.concatenate([updated, extra], axis=0).astype(BF16)


def routes(homes, old_home, old_extra, new_home, new_extra):
    me = lax.axis_index("expert")
    my_old = lax.dynamic_slice_in_dim(old_home, me * homes, homes)
    my_new = lax.dynamic_slice_in_dim(new_home, me * homes, homes)
    wanted = lax.dynamic_slice_in_dim(new_extra, me, 1)
    ids = jnp.arange(homes, dtype=jnp.int32)
    changed = my_old != my_new
    slot = jnp.sum(jnp.where(changed, ids, 0))
    arriving = jnp.sum(jnp.where(changed, my_new, 0))
    owner = jnp.arange(old_home.shape[0], dtype=jnp.int32) // homes
    source = jnp.sum(jnp.where(old_home == arriving, owner, 0))
    extra_source = jnp.sum(jnp.where(old_home == wanted, owner, 0))
    asked = jnp.sum(jnp.where(new_extra[:, None] == my_old[None, :], ids[None, :], 0), axis=1)
    adds = jnp.sum(jnp.where(old_extra[:, None] == my_new[None, :], ids[None, :] + 1, 0), axis=1) - 1
    extra_adds = (old_extra == wanted).astype(jnp.int32)
    head = jnp.stack([slot, source, extra_source] + [slot] * 5)
    return jnp.concatenate([head, asked, adds, extra_adds])


def per_device(grads, weights, first, second, old_home, old_extra, new_home, new_extra):
    homes, width = weights.shape
    tiles = width // LANES
    outer = lax.axis_size("outer")
    devices = lax.axis_size("expert")
    scal = routes(homes, old_home, old_extra, new_home, new_extra)
    states = pl.pallas_call(
        state_kernel,
        in_specs=[SMEM, VMEM, VMEM, VMEM],
        out_specs=VMEM,
        out_shape=jax.ShapeDtypeStruct((devices, 6 * ROW, LANES), F32),
        scratch_shapes=[pltpu.VMEM((homes, 3 * ROW, LANES), F32)],
        compiler_params=pltpu.CompilerParams(vmem_limit_bytes=16 * 2**20),
        cost_estimate=cost(1 << 18),
    )(scal, weights, first, second)
    early = lax.all_to_all(states.astype(F16), "expert", 0, 0, tiled=True)
    halves = split_by_core(grads, outer, width)
    pair = lax.all_to_all(halves, "core", 0, 0, tiled=True).astype(F32)
    partial = ((pair[0] + pair[1]) * PAIR_SCALE).astype(F16)
    parts = lax.all_to_all(partial, "outer", 0, 0, tiled=True)
    sums = jnp.sum(parts.astype(F32), axis=0) * (1.0 / PAIR_SCALE)
    outgoing = pl.pallas_call(
        sums_kernel,
        in_specs=[SMEM, VMEM],
        out_specs=VMEM,
        out_shape=jax.ShapeDtypeStruct((devices, 3 * ROW, LANES), F32),
        scratch_shapes=[pltpu.VMEM((homes, ROW, LANES), F32)],
        compiler_params=pltpu.CompilerParams(vmem_limit_bytes=16 * 2**20),
        cost_estimate=cost(1 << 18),
    )(scal, sums)
    late = lax.all_to_all((outgoing * SUM_SCALE).astype(F16), "expert", 0, 0, tiled=True)
    late = late.astype(F32) * (1.0 / SUM_SCALE)
    moved = lax.dynamic_slice(early, (scal[1], 0, 0), (1, 3 * ROW, LANES))
    copied = lax.dynamic_slice(early, (scal[2], 3 * ROW, 0), (1, 3 * ROW, LANES))
    state = jnp.concatenate([moved, copied], axis=1).astype(F32) * (1.0 / STATE_SCALE)
    state = state.reshape(6, ROW, LANES)[:, :tiles, :].reshape(6, width)
    return pl.pallas_call(
        final_kernel,
        in_specs=[SMEM] + [VMEM] * 6,
        out_specs=[VMEM] * 3,
        out_shape=[
            jax.ShapeDtypeStruct((homes + 1, width), BF16),
            jax.ShapeDtypeStruct((homes, width), F32),
            jax.ShapeDtypeStruct((homes, width), F32),
        ],
        scratch_shapes=[pltpu.VMEM((homes + 1, ROW, LANES), F32), pltpu.VMEM((ROW, width), F32)],
        compiler_params=pltpu.CompilerParams(vmem_limit_bytes=16 * 2**20),
        cost_estimate=cost(1 << 18),
    )(scal, sums, late, state, weights, first, second)


def solution(mesh):
    groups, devices = mesh.devices.shape
    grid = Mesh(mesh.devices.reshape(groups // 2, 2, devices), ("outer", "core", "expert"))
    dp = ("outer", "core")
    placed = (P(dp, "expert", None), P("expert", dp), P("expert", dp), P("expert", dp), P(), P(), P(), P())
    return jax.shard_map(
        per_device,
        mesh=grid,
        in_specs=placed,
        out_specs=(P("expert", dp), P("expert", dp), P("expert", dp)),
        check_vma=False,
    )
```

time: 582 us -> 102 us (0.18)
  blocking collectives: 390 us -> 4.58 us
  waiting for transfers between devices: 162 us -> 38.4 us
  starting transfers between devices: 0.04 us -> 36 us
  between operations: 16.2 us -> 4.59 us
    all_gather x5 -> x0, blocking collectives: 390 us -> none  [the longest x1 81.2 us: per_device(): piece = lax.all_gather(updated, 'expert', axis=0, tiled=True)]
    reduce_scatter x1 -> x0, waiting for transfers between devices: 162 us -> none  [per_device(): lax.psum_scatter(grads[0].astype(jnp.float32), 'dp', scatter_dimension=1,...]
    all_to_all x0 -> x3, waiting for transfers between devices: none -> 38.4 us  [the longest x1 19.6 us: per_device(): early = lax.all_to_all(states.astype(F16), 'expert', 0, 0, tiled=True)]
    all_to_all x0 -> x3, starting transfers between devices: none -> 36 us  [the longest x1 16.4 us: per_device(): parts = lax.all_to_all(partial, 'outer', 0, 0, tiled=True)]
  transfers between devices with their start and end apart: 1 -> 3, of which waited for: 1 -> 3; matrix products, arithmetic and copies ran while one was open for 1% -> 11% of each run, Pallas kernels for 0% -> 1%
where the time goes in v1:
time: 102 us; the launch traced here: 101 us
  waiting for transfers between devices  38.4 us (38%)
  starting transfers between devices  36 us (35%)
  local copies, waits for them, and re-layouts  7.37 us (7%)
  other arithmetic  6.66 us (7%)
  between operations  4.59 us (4%)
  blocking collectives  4.58 us (4%)
  Pallas kernels  3.77 us (4%)
    all_to_all x1, waiting for transfers between devices, per_device(): early = lax.all_to_all(states.astype(F16), 'expert', 0, 0, tiled=True)  19.6 us
    all_to_all x1, starting transfers between devices, per_device(): parts = lax.all_to_all(partial, 'outer', 0, 0, tiled=True)  16.4 us
    all_to_all x1, starting transfers between devices, per_device(): early = lax.all_to_all(states.astype(F16), 'expert', 0, 0, tiled=True)  13.9 us
    all_to_all x1, waiting for transfers between devices, per_device(): lax.all_to_all((outgoing * SUM_SCALE).astype(F16), 'expert', 0, 0, tiled=...  10.5 us
    all_to_all x1, waiting for transfers between devices, per_device(): parts = lax.all_to_all(partial, 'outer', 0, 0, tiled=True)  8.24 us
    all_to_all x1, starting transfers between devices, per_device(): lax.all_to_all((outgoing * SUM_SCALE).astype(F16), 'expert', 0, 0, tiled=...  5.63 us
    concatenate x1, local copies, waits for them, and re-layouts, routes(): return jnp.concatenate([head, asked, adds, extra_adds])  5.21 us
    all_to_all x1, blocking collectives, per_device(): pair = lax.all_to_all(halves, 'core', 0, 0, tiled=True).astype(F32)  4.58 us
  transfers between devices with their start and end apart: 3, of which 3 were waited for; matrix products, arithmetic and copies ran while one was open for 11% of the time, Pallas kernels for 1%

profile of v1, /device:TPU:14, one launch (start us, length us, event | category | flops | bytes accessed | tf_op | source)
XLA Modules:
  0.0 101.3 jit_solution(11212514946710656138)
XLA Ops:
  0.6 0.0 copy-start
  0.6 1.5 %copy-done = bf16[1,9,57344]{2,1,0:T(8,128)(2,1)S(1)} copy-done((bf16[1,9,57344]{2,1,0:T(8,128)(2,1)S(1)}, bf16[1,9,57344]{2,1,0:T(8,128)(2,1)}, u32[]{:S(2)}) %copy-start) | copy-done | bytes 1032216
  2.1 0.6 shard_map.103
  2.7 4.6 %all_to_all.20 = bf16[2,16,128,128]{3,2,1,0:T(8,128)(2,1)S(1)} all-to-all(bf16[2,16,128,128]{3,2,1,0:T(8,128)(2,1)S(1)} %shard_map.103), channel_id=1, replica_groups=mesh['outer'=16,'core'=2,'expert'=32] {'core'}, dimensions={0} | all-to-all | bytes 2097152 | tf_op jit(solution)/shard_map/all_to_all | solution.py:169
  7.3 0.2 convert_element_type.32
  7.5 0.0 copy-start.7
  7.5 0.0 copy-start.4
  7.6 0.0 copy-start.6
  7.6 0.0 copy-start.5
  7.6 0.0 copy-start.1
  7.6 0.0 copy-start.2
  7.6 0.0 copy-start.3
  7.6 1.0 fusion.2
  8.6 16.4 %all-to-all-start.1 = ((f16[16,128,128]{2,1,0:T(8,128)(2,1)}), f16[16,128,128]{2,1,0:T(8,128)(2,1)S(1)}, u32[]{:S(2)}, u32[]{:S(2)}) async-start(f16[16,128,128]{2,1,0:T(8,128)(2,1)} %fusion.2), calls=%async_computation.1 | async-start | bytes 1048576 | tf_op jit(solution)/shard_map/all_to_all | solution.py:171
  25.0 0.0 copy-done.7
  25.0 0.6 dynamic_slice.17
  25.6 0.0 copy-done.4
  25.6 0.0 copy-done.6
  25.6 0.7 fusion.6
  26.3 2.0 %fusion.4 = (s32[]{:T(128)}, s32[]{:T(128)}) fusion(s32[256]{0:T(256)S(1)} %copy-done.4, s32[]{:T(128)} %bitcast.2, s32[]{:T(128)} %get-tuple-element.5), kind=kLoop, calls=%fused_computation.23 | loop fusion | flops 3582 | bytes 1040 | tf_op jit(solution)/shard_map/reduce_sum | solution.py:144
  28.3 0.1 select_reduce_fusion.1
  28.3 0.0 copy-done.5
  28.3 0.1 select_reduce_fusion
  28.4 0.6 compare_convert_fusion
  29.1 5.2 %concatenate.8.scal = s32[104]{0:T(128)S(1)} concatenate(s32[1]{0:T(128)} %bitcast, s32[1]{0:T(128)} %bitcast.1, s32[1]{0:T(128)} %bitcast.3, s32[1]{0:T(128)} %bitcast, s32[1]{0:T(128)} %bitcast, s32[1]{0:T(128)} %bitcast, s32[1]{0:T(128)} %bitcast, s32[1]{0:T(128)} %bitcast, s32[32]{0:T(128)S(1)} %select_reduce_fusion.1, s32[32]{0:T(128)S(1)} %broadcast_add_fusion, ...), dimensions={0} | concatenate | bytes 832 | tf_op jit(solution)/shard_map/concatenate | solution.py:149
  34.3 0.0 copy-done.1
  34.3 0.0 copy-done.2
  34.3 0.0 copy-done.3
  34.3 0.7 shard_map.105
  35.0 1.0 convert_element_type.38
  36.0 8.2 %all-to-all-done.1 = f16[16,128,128]{2,1,0:T(8,128)(2,1)S(1)} async-done(((f16[16,128,128]{2,1,0:T(8,128)(2,1)}), f16[16,128,128]{2,1,0:T(8,128)(2,1)S(1)}, u32[]{:S(2)}, u32[]{:S(2)}) %all-to-all-start.1) | async-done | bytes 524320 | tf_op jit(solution)/shard_map/all_to_all | solution.py:171
  44.3 13.9 %all-to-all-start.3 = ((f16[32,96,128]{2,1,0:T(8,128)(2,1)}), f16[32,96,128]{2,1,0:T(8,128)(2,1)S(1)}, u32[]{:S(2)}, u32[]{:S(2)}) async-start(f16[32,96,128]{2,1,0:T(8,128)(2,1)} %convert_element_type.38), calls=%async_computation.3 | async-start | bytes 1572864 | tf_op jit(solution)/shard_map/all_to_all | solution.py:167
  58.2 0.1 convert_reduce_fusion
  58.3 0.6 shard_map.104
  58.9 0.8 multiply_convert_fusion
  59.8 19.6 %all-to-all-done.3 = f16[32,96,128]{2,1,0:T(8,128)(2,1)S(1)} async-done(((f16[32,96,128]{2,1,0:T(8,128)(2,1)}), f16[32,96,128]{2,1,0:T(8,128)(2,1)S(1)}, u32[]{:S(2)}, u32[]{:S(2)}) %all-to-all-start.3) | async-done | bytes 786464 | tf_op jit(solution)/shard_map/all_to_all | solution.py:167
  79.4 5.6 %all-to-all-start.2 = ((f16[32,48,128]{2,1,0:T(8,128)(2,1)}), f16[32,48,128]{2,1,0:T(8,128)(2,1)S(1)}, u32[]{:S(2)}, u32[]{:S(2)}) async-start(f16[32,48,128]{2,1,0:T(8,128)(2,1)} %multiply_convert_fusion), calls=%async_computation.2 | async-start | bytes 786432 | tf_op jit(solution)/shard_map/all_to_all | solution.py:182
  88.9 10.5 %all-to-all-done.2 = f16[32,48,128]{2,1,0:T(8,128)(2,1)S(1)} async-done(((f16[32,48,128]{2,1,0:T(8,128)(2,1)}), f16[32,48,128]{2,1,0:T(8,128)(2,1)S(1)}, u32[]{:S(2)}, u32[]{:S(2)}) %all-to-all-start.2) | async-done | bytes 393248 | tf_op jit(solution)/shard_map/all_to_all | solution.py:182
  99.4 0.1 convert_multiply_fusion.late_ref
  99.5 1.9 %shard_map.106 = (bf16[9,1792]{1,0:T(8,128)(2,1)}, f32[8,1792]{1,0:T(8,128)}, f32[8,1792]{1,0:T(8,128)}) custom-call(s32[104]{0:T(128)S(1)} %concatenate.8.scal, f32[128,128]{1,0:T(8,128)S(1)} %broadcast_multiply_fusion.s_ref.sums_ref, f32[32,48,128]{2,1,0:T(8,128)S(1)} %convert_multiply_fusion.late_ref, f32[6,1792]{1,0:T(8,128)S(1)} %bitcast.12, ...), custom_call_target="tpu_custom_call" | custom-call | flops 262144 | bytes 1048576 | tf_op jit(solution)/shard_map/pallas_call | solution.py:188
  (6 shorter events, 0.1 us)
Async XLA Ops:
  0.6 1.5 %copy-start = (bf16[1,9,57344]{2,1,0:T(8,128)(2,1)S(1)}, bf16[1,9,57344]{2,1,0:T(8,128)(2,1)}, u32[]{:S(2)}) copy-start(bf16[1,9,57344]{2,1,0:T(8,128)(2,1)} %refs_0_.1) | copy-start | bytes 3096580
  7.5 17.5 %copy-start.7 = (s32[32]{0:T(128)S(1)}, s32[32]{0:T(128)}, u32[]{:S(2)}) copy-start(s32[32]{0:T(128)} %param.15) | copy-start | bytes 388
  7.5 18.0 %copy-start.4 = (s32[256]{0:T(256)S(1)}, s32[256]{0:T(256)}, u32[]{:S(2)}) copy-start(s32[256]{0:T(256)} %param.12) | copy-start | bytes 3076
  7.6 18.0 %copy-start.6 = (s32[256]{0:T(256)S(1)}, s32[256]{0:T(256)}, u32[]{:S(2)}) copy-start(s32[256]{0:T(256)} %param.14) | copy-start | bytes 3076
  7.6 20.8 %copy-start.5 = (s32[32]{0:T(128)S(1)}, s32[32]{0:T(128)}, u32[]{:S(2)}) copy-start(s32[32]{0:T(128)} %param.13) | copy-start | bytes 388
  7.6 26.7 %copy-start.1 = (f32[8,1792]{1,0:T(8,128)S(1)}, f32[8,1792]{1,0:T(8,128)}, u32[]{:S(2)}) copy-start(f32[8,1792]{1,0:T(8,128)} %f_ref.3) | copy-start | bytes 172036
  7.6 26.7 %copy-start.2 = (f32[8,1792]{1,0:T(8,128)S(1)}, f32[8,1792]{1,0:T(8,128)}, u32[]{:S(2)}) copy-start(f32[8,1792]{1,0:T(8,128)} %s_ref.3) | copy-start | bytes 172036
  7.6 26.7 %copy-start.3 = (bf16[8,1792]{1,0:T(8,128)(2,1)S(1)}, bf16[8,1792]{1,0:T(8,128)(2,1)}, u32[]{:S(2)}) copy-start(bf16[8,1792]{1,0:T(8,128)(2,1)} %w_ref.3) | copy-start | bytes 86020
  8.6 35.7 %all-to-all-start.1 = ((f16[16,128,128]{2,1,0:T(8,128)(2,1)}), f16[16,128,128]{2,1,0:T(8,128)(2,1)S(1)}, u32[]{:S(2)}, u32[]{:S(2)}) async-start(f16[16,128,128]{2,1,0:T(8,128)(2,1)} %fusion.2), calls=%async_computation.1 | async-start | bytes 1048576 | tf_op jit(solution)/shard_map/all_to_all | solution.py:171
  44.3 35.1 %all-to-all-start.3 = ((f16[32,96,128]{2,1,0:T(8,128)(2,1)}), f16[32,96,128]{2,1,0:T(8,128)(2,1)S(1)}, u32[]{:S(2)}, u32[]{:S(2)}) async-start(f16[32,96,128]{2,1,0:T(8,128)(2,1)} %convert_element_type.38), calls=%async_computation.3 | async-start | bytes 1572864 | tf_op jit(solution)/shard_map/all_to_all | solution.py:167
  79.4 20.0 %all-to-all-start.2 = ((f16[32,48,128]{2,1,0:T(8,128)(2,1)}), f16[32,48,128]{2,1,0:T(8,128)(2,1)S(1)}, u32[]{:S(2)}, u32[]{:S(2)}) async-start(f16[32,48,128]{2,1,0:T(8,128)(2,1)} %multiply_convert_fusion), calls=%async_computation.2 | async-start | bytes 786432 | tf_op jit(solution)/shard_map/all_to_all | solution.py:182

commit v2 on v1

--- a/solution.py
+++ b/solution.py
@@ -57,34 +57,27 @@
     )(grads)
 
 
-def state_kernel(scal, w_ref, f_ref, s_ref, out_ref, rows):
+def rows_kernel(scal, sums_ref, w_ref, f_ref, s_ref, out_ref, rows):
     homes, width = f_ref.shape
     tiles = width // LANES
-    rows[...] = jnp.zeros_like(rows)
     for n, ref in enumerate((w_ref, f_ref, s_ref)):
         value = ref[...].astype(F32) * STATE_SCALE
         for i in range(homes):
             for t in range(tiles):
-                rows[i, n * ROW + t : n * ROW + t + 1, :] = value[i : i + 1, t * LANES : (t + 1) * LANES]
-    leaving = rows[scal[0]]
-    for d in range(out_ref.shape[0]):
-        out_ref[d, : 3 * ROW, :] = leaving
-        out_ref[d, 3 * ROW :, :] = rows[scal[8 + d]]
-
-
-def sums_kernel(scal, s_ref, out_ref, rows):
-    homes = rows.shape[0]
-    tiles = (s_ref.shape[0] - ROW) // homes
-    rows[...] = jnp.zeros_like(rows)
+                at = n * tiles + t
+                rows[i, at : at + 1, :] = value[i : i + 1, t * LANES : (t + 1) * LANES]
+    sums = sums_ref[...] * SUM_SCALE
     for i in range(homes):
         for t in range(tiles):
-            rows[i, t : t + 1, :] = s_ref[t * homes + i : t * homes + i + 1, :]
-    extra = s_ref[tiles * homes :, :]
+            at = 3 * tiles + t
+            rows[i, at : at + 1, :] = sums[t * homes + i : t * homes + i + 1, :]
+    extra = sums[tiles * homes :, :]
     leaving = rows[scal[0]]
+    per = 4 * tiles
     for d in range(out_ref.shape[0]):
-        out_ref[d, :ROW, :] = extra
-        out_ref[d, ROW : 2 * ROW, :] = leaving
-        out_ref[d, 2 * ROW :, :] = rows[scal[8 + d]]
+        out_ref[d, :per, :] = leaving
+        out_ref[d, per : 2 * per, :] = rows[scal[8 + d]]
+        out_ref[d, 2 * per :, :] = extra
 
 
 def adam(total, base, first, second):
@@ -94,37 +87,43 @@
     return base - 0.02 * (step + 0.1 * base), moment1, moment2
 
 
-def final_kernel(scal, sums_ref, late_ref, early_ref, w_ref, f_ref, s_ref, nw_ref, nf_ref, ns_ref, acc, flat):
+def final_kernel(scal, sums_ref, extras_ref, got_ref, w_ref, f_ref, s_ref, nw_ref, nf_ref, ns_ref, acc, flat):
     homes, width = f_ref.shape
     tiles = width // LANES
-    devices = late_ref.shape[0]
+    devices = extras_ref.shape[0]
     slot = scal[0]
     acc[...] = jnp.zeros_like(acc)
-    acc[slot] = late_ref[scal[1], ROW : 2 * ROW, :]
-    acc[homes] = late_ref[scal[2], 2 * ROW :, :]
     for s in range(devices):
         to = scal[8 + devices + s]
 
         @pl.when(to >= 0)
         def _():
-            acc[to] += late_ref[s, :ROW, :]
+            acc[to] += extras_ref[s]
 
         @pl.when(scal[8 + 2 * devices + s] > 0)
         def _():
-            acc[homes] += late_ref[s, :ROW, :]
+            acc[homes] += extras_ref[s]
 
     for t in range(tiles):
+        cols = slice(t * LANES, (t + 1) * LANES)
         for i in range(homes + 1):
-            flat[i : i + 1, t * LANES : (t + 1) * LANES] = acc[i, t : t + 1, :]
+            flat[i : i + 1, cols] = acc[i, t : t + 1, :]
+        for n in range(8):
+            at = n * tiles + t
+            flat[2 * homes + n : 2 * homes + n + 1, cols] = got_ref[at : at + 1, :]
     is_new = lax.broadcasted_iota(jnp.int32, (homes, LANES), 0) == slot
     for t in range(tiles):
         cols = slice(t * LANES, (t + 1) * LANES)
-        total = flat[:homes, cols] + jnp.where(is_new, 0.0, sums_ref[t * homes : (t + 1) * homes, :])
-        base = jnp.where(is_new, early_ref[0:1, cols], w_ref[:, cols].astype(F32))
-        first = jnp.where(is_new, early_ref[1:2, cols], f_ref[:, cols])
-        second = jnp.where(is_new, early_ref[2:3, cols], s_ref[:, cols])
+        got = flat[2 * homes : 2 * homes + 8, cols]
+        own = sums_ref[t * homes : (t + 1) * homes, :]
+        total = (flat[:homes, cols] + jnp.where(is_new, got[3:4], own * SUM_SCALE)) * (1.0 / SUM_SCALE)
+        base = jnp.where(is_new, got[0:1] * (1.0 / STATE_SCALE), w_ref[:, cols].astype(F32))
+        first = jnp.where(is_new, got[1:2] * (1.0 / STATE_SCALE), f_ref[:, cols])
+        second = jnp.where(is_new, got[2:3] * (1.0 / STATE_SCALE), s_ref[:, cols])
         updated, moment1, moment2 = adam(total, base, first, second)
-        extra, _, _ = adam(flat[homes : homes + 1, cols], early_ref[3:4, cols], early_ref[4:5, cols], early_ref[5:6, cols])
+        total = (flat[homes : homes + 1, cols] + got[7:8]) * (1.0 / SUM_SCALE)
+        state = got * (1.0 / STATE_SCALE)
+        extra, _, _ = adam(total, state[4:5], state[5:6], state[6:7])
         nf_ref[:, cols] = moment1
         ns_ref[:, cols] = moment2
         nw_ref[:, cols] = jnp.concatenate([updated, extra], axis=0).astype(BF16)
@@ -155,36 +154,25 @@
     outer = lax.axis_size("outer")
     devices = lax.axis_size("expert")
     scal = routes(homes, old_home, old_extra, new_home, new_extra)
-    states = pl.pallas_call(
-        state_kernel,
-        in_specs=[SMEM, VMEM, VMEM, VMEM],
-        out_specs=VMEM,
-        out_shape=jax.ShapeDtypeStruct((devices, 6 * ROW, LANES), F32),
-        scratch_shapes=[pltpu.VMEM((homes, 3 * ROW, LANES), F32)],
-        compiler_params=pltpu.CompilerParams(vmem_limit_bytes=16 * 2**20),
-        cost_estimate=cost(1 << 18),
-    )(scal, weights, first, second)
-    early = lax.all_to_all(states.astype(F16), "expert", 0, 0, tiled=True)
     halves = split_by_core(grads, outer, width)
     pair = lax.all_to_all(halves, "core", 0, 0, tiled=True).astype(F32)
     partial = ((pair[0] + pair[1]) * PAIR_SCALE).astype(F16)
     parts = lax.all_to_all(partial, "outer", 0, 0, tiled=True)
     sums = jnp.sum(parts.astype(F32), axis=0) * (1.0 / PAIR_SCALE)
     outgoing = pl.pallas_call(
-        sums_kernel,
-        in_specs=[SMEM, VMEM],
+        rows_kernel,
+        in_specs=[SMEM] + [VMEM] * 4,
         out_specs=VMEM,
-        out_shape=jax.ShapeDtypeStruct((devices, 3 * ROW, LANES), F32),
-        scratch_shapes=[pltpu.VMEM((homes, ROW, LANES), F32)],
+        out_shape=jax.ShapeDtypeStruct((devices, 8 * tiles + ROW, LANES), F32),
+        scratch_shapes=[pltpu.VMEM((homes, 4 * tiles, LANES), F32)],
         compiler_params=pltpu.CompilerParams(vmem_limit_bytes=16 * 2**20),
         cost_estimate=cost(1 << 18),
-    )(scal, sums)
-    late = lax.all_to_all((outgoing * SUM_SCALE).astype(F16), "expert", 0, 0, tiled=True)
-    late = late.astype(F32) * (1.0 / SUM_SCALE)
-    moved = lax.dynamic_slice(early, (scal[1], 0, 0), (1, 3 * ROW, LANES))
-    copied = lax.dynamic_slice(early, (scal[2], 3 * ROW, 0), (1, 3 * ROW, LANES))
-    state = jnp.concatenate([moved, copied], axis=1).astype(F32) * (1.0 / STATE_SCALE)
-    state = state.reshape(6, ROW, LANES)[:, :tiles, :].reshape(6, width)
+    )(scal, sums, weights, first, second)
+    arrived = lax.all_to_all(outgoing.astype(F16), "expert", 0, 0, tiled=True)
+    extras = arrived[:, 8 * tiles :, :].astype(F32)
+    moved = lax.dynamic_slice(arrived, (scal[1], 0, 0), (1, 4 * tiles, LANES))
+    copied = lax.dynamic_slice(arrived, (scal[2], 4 * tiles, 0), (1, 4 * tiles, LANES))
+    got = jnp.concatenate([moved[0], copied[0]], axis=0).astype(F32)
     return pl.pallas_call(
         final_kernel,
         in_specs=[SMEM] + [VMEM] * 6,
@@ -194,10 +182,10 @@
             jax.ShapeDtypeStruct((homes, width), F32),
             jax.ShapeDtypeStruct((homes, width), F32),
         ],
-        scratch_shapes=[pltpu.VMEM((homes + 1, ROW, LANES), F32), pltpu.VMEM((ROW, width), F32)],
+        scratch_shapes=[pltpu.VMEM((homes + 1, ROW, LANES), F32), pltpu.VMEM((3 * homes, width), F32)],
         compiler_params=pltpu.CompilerParams(vmem_limit_bytes=16 * 2**20),
         cost_estimate=cost(1 << 18),
-    )(scal, sums, late, state, weights, first, second)
+    )(scal, sums, extras, got, weights, first, second)
 
 
 def solution(mesh):

time: 102 us -> 89.9 us (0.88)
  waiting for transfers between devices: 38.4 us -> 32.5 us
  starting transfers between devices: 36 us -> 30.3 us
    all_to_all x2 -> x1, waiting for transfers between devices: 30.1 us -> 22.6 us  [per_device(): arrived = lax.all_to_all(outgoing.astype(F16), 'expert', 0, 0, tiled=True)]
    all_to_all x2 -> x1, starting transfers between devices: 19.6 us -> 13.9 us  [per_device(): arrived = lax.all_to_all(outgoing.astype(F16), 'expert', 0, 0, tiled=True)]
    all_to_all x1, waiting for transfers between devices: 8.24 us -> 9.92 us  [per_device(): parts = lax.all_to_all(partial, 'outer', 0, 0, tiled=True)]
  transfers between devices with their start and end apart: 3 -> 2, of which waited for: 3 -> 2; matrix products, arithmetic and copies ran while one was open for 11% -> 11% of each run, Pallas kernels for 1% -> 0%
where the time goes in v2:
time: 89.9 us; the launch traced here: 88.6 us
  waiting for transfers between devices  32.5 us (36%)
  starting transfers between devices  30.3 us (34%)
  local copies, waits for them, and re-layouts  7.35 us (8%)
  other arithmetic  6.03 us (7%)
  blocking collectives  4.58 us (5%)
  between operations  4.55 us (5%)
  Pallas kernels  3.26 us (4%)
    all_to_all x1, waiting for transfers between devices, per_device(): arrived = lax.all_to_all(outgoing.astype(F16), 'expert', 0, 0, tiled=True)  22.6 us
    all_to_all x1, starting transfers between devices, per_device(): parts = lax.all_to_all(partial, 'outer', 0, 0, tiled=True)  16.4 us
    all_to_all x1, starting transfers between devices, per_device(): arrived = lax.all_to_all(outgoing.astype(F16), 'expert', 0, 0, tiled=True)  13.9 us
    all_to_all x1, waiting for transfers between devices, per_device(): parts = lax.all_to_all(partial, 'outer', 0, 0, tiled=True)  9.92 us
    concatenate x1, local copies, waits for them, and re-layouts, routes(): return jnp.concatenate([head, asked, adds, extra_adds])  5.2 us
    all_to_all x1, blocking collectives, per_device(): pair = lax.all_to_all(halves, 'core', 0, 0, tiled=True).astype(F32)  4.58 us
    reduce_sum x1, other arithmetic, routes(): extra_source = jnp.sum(jnp.where(old_home == wanted, owner, 0))  2 us
    pallas_call x1, Pallas kernels, per_device(): pl.pallas_call(final_kernel, in_specs=[SMEM] + [VMEM] * 6, out_specs=[VME...  1.93 us
  transfers between devices with their start and end apart: 2, of which 2 were waited for; matrix products, arithmetic and copies ran while one was open for 11% of the time, Pallas kernels for 0%

profile of v2, /device:TPU:14, one launch (start us, length us, event | category | flops | bytes accessed | tf_op | source)
XLA Modules:
  0.0 88.6 jit_solution(14333170612496770552)
XLA Ops:
  0.6 0.0 copy-start
  0.6 1.5 %copy-done = bf16[1,9,57344]{2,1,0:T(8,128)(2,1)S(1)} copy-done((bf16[1,9,57344]{2,1,0:T(8,128)(2,1)S(1)}, bf16[1,9,57344]{2,1,0:T(8,128)(2,1)}, u32[]{:S(2)}) %copy-start) | copy-done | bytes 1032216
  2.1 0.6 shard_map.103
  2.7 4.6 %all_to_all.15 = bf16[2,16,128,128]{3,2,1,0:T(8,128)(2,1)S(1)} all-to-all(bf16[2,16,128,128]{3,2,1,0:T(8,128)(2,1)S(1)} %shard_map.103), channel_id=1, replica_groups=mesh['outer'=16,'core'=2,'expert'=32] {'core'}, dimensions={0} | all-to-all | bytes 2097152 | tf_op jit(solution)/shard_map/all_to_all | solution.py:158
  7.3 0.2 convert_element_type.25
  7.5 0.0 copy-start.7
  7.5 0.0 copy-start.4
  7.6 0.0 copy-start.6
  7.6 0.0 copy-start.5
  7.6 0.0 copy-start.1
  7.6 0.0 copy-start.2
  7.6 0.0 copy-start.3
  7.6 1.0 %fusion.2 = f16[16,128,128]{2,1,0:T(8,128)(2,1)} fusion(f32[2,16,128,128]{3,2,1,0:T(8,128)S(1)} %convert_element_type.25), kind=kLoop, calls=%fused_computation.4 | loop fusion | flops 786432 | bytes 2621440 | tf_op jit(solution)/shard_map/convert_element_type | solution.py:159
  8.6 16.4 %all-to-all-start.1 = ((f16[16,128,128]{2,1,0:T(8,128)(2,1)}), f16[16,128,128]{2,1,0:T(8,128)(2,1)S(1)}, u32[]{:S(2)}, u32[]{:S(2)}) async-start(f16[16,128,128]{2,1,0:T(8,128)(2,1)} %fusion.2), calls=%async_computation.1 | async-start | bytes 1048576 | tf_op jit(solution)/shard_map/all_to_all | solution.py:160
  25.0 0.0 copy-done.7
  25.0 0.6 dynamic_slice.17
  25.6 0.0 copy-done.4
  25.6 0.0 copy-done.6
  25.6 0.7 fusion.6
  26.3 2.0 %fusion.4 = (s32[]{:T(128)}, s32[]{:T(128)}) fusion(s32[256]{0:T(256)S(1)} %copy-done.4, s32[]{:T(128)} %bitcast.2, s32[]{:T(128)} %get-tuple-element.5), kind=kLoop, calls=%fused_computation.22 | loop fusion | flops 3582 | bytes 1040 | tf_op jit(solution)/shard_map/reduce_sum | solution.py:143
  28.3 0.1 select_reduce_fusion.1
  28.4 0.0 copy-done.5
  28.4 0.1 select_reduce_fusion
  28.5 0.6 compare_convert_fusion
  29.1 5.2 %concatenate.6.scal = s32[104]{0:T(128)S(1)} concatenate(s32[1]{0:T(128)} %bitcast, s32[1]{0:T(128)} %bitcast.1, s32[1]{0:T(128)} %bitcast.3, s32[1]{0:T(128)} %bitcast, s32[1]{0:T(128)} %bitcast, s32[1]{0:T(128)} %bitcast, s32[1]{0:T(128)} %bitcast, s32[1]{0:T(128)} %bitcast, s32[32]{0:T(128)S(1)} %select_reduce_fusion.1, s32[32]{0:T(128)S(1)} %broadcast_add_fusion, ...), dimensions={0} | concatenate | bytes 832 | tf_op jit(solution)/shard_map/concatenate | solution.py:148
  34.3 9.9 %all-to-all-done.1 = f16[16,128,128]{2,1,0:T(8,128)(2,1)S(1)} async-done(((f16[16,128,128]{2,1,0:T(8,128)(2,1)}), f16[16,128,128]{2,1,0:T(8,128)(2,1)S(1)}, u32[]{:S(2)}, u32[]{:S(2)}) %all-to-all-start.1) | async-done | bytes 524320 | tf_op jit(solution)/shard_map/all_to_all | solution.py:160
  44.3 0.1 convert_reduce_fusion
  44.4 0.0 copy-done.1
  44.4 0.0 copy-done.2
  44.4 0.0 copy-done.3
  44.4 0.8 shard_map.104
  45.1 1.2 %convert_element_type.29 = f16[32,128,128]{2,1,0:T(8,128)(2,1)} convert(f32[32,128,128]{2,1,0:T(8,128)S(1)} %shard_map.104) | non-fusion elementwise | flops 524288 | bytes 3145728 | tf_op jit(solution)/shard_map/convert_element_type | solution.py:171
  46.3 13.9 %all-to-all-start.2 = ((f16[32,128,128]{2,1,0:T(8,128)(2,1)}), f16[32,128,128]{2,1,0:T(8,128)(2,1)S(1)}, u32[]{:S(2)}, u32[]{:S(2)}) async-start(f16[32,128,128]{2,1,0:T(8,128)(2,1)} %convert_element_type.29), calls=%async_computation.2 | async-start | bytes 2097152 | tf_op jit(solution)/shard_map/all_to_all | solution.py:171
  64.0 22.6 %all-to-all-done.2 = f16[32,128,128]{2,1,0:T(8,128)(2,1)S(1)} async-done(((f16[32,128,128]{2,1,0:T(8,128)(2,1)}), f16[32,128,128]{2,1,0:T(8,128)(2,1)S(1)}, u32[]{:S(2)}, u32[]{:S(2)}) %all-to-all-start.2) | async-done | bytes 1048608 | tf_op jit(solution)/shard_map/all_to_all | solution.py:171
  86.7 1.9 %shard_map.105 = (bf16[9,1792]{1,0:T(8,128)(2,1)}, f32[8,1792]{1,0:T(8,128)}, f32[8,1792]{1,0:T(8,128)}) custom-call(s32[104]{0:T(128)S(1)} %concatenate.6.scal, f32[128,128]{1,0:T(8,128)S(1)} %broadcast_multiply_fusion.sums_ref, f32[32,16,128]{2,1,0:T(8,128)S(1)} %slice_convert_fusion.extras_ref, f32[112,128]{1,0:T(8,128)S(1)} %maximum_convert_fusion.got_ref, ...), custom_call_target="tpu_custom_call" | custom-call | flops 262144 | bytes 1048576 | tf_op jit(solution)/shard_map/pallas_call | solution.py:176
  (5 shorter events, 0.1 us)
Async XLA Ops:
  0.6 1.5 %copy-start = (bf16[1,9,57344]{2,1,0:T(8,128)(2,1)S(1)}, bf16[1,9,57344]{2,1,0:T(8,128)(2,1)}, u32[]{:S(2)}) copy-start(bf16[1,9,57344]{2,1,0:T(8,128)(2,1)} %refs_0_.1) | copy-start | bytes 3096580
  7.5 17.5 %copy-start.7 = (s32[32]{0:T(128)S(1)}, s32[32]{0:T(128)}, u32[]{:S(2)}) copy-start(s32[32]{0:T(128)} %param.15) | copy-start | bytes 388
  7.5 18.0 %copy-start.4 = (s32[256]{0:T(256)S(1)}, s32[256]{0:T(256)}, u32[]{:S(2)}) copy-start(s32[256]{0:T(256)} %param.12) | copy-start | bytes 3076
  7.6 18.0 %copy-start.6 = (s32[256]{0:T(256)S(1)}, s32[256]{0:T(256)}, u32[]{:S(2)}) copy-start(s32[256]{0:T(256)} %param.14) | copy-start | bytes 3076
  7.6 20.8 %copy-start.5 = (s32[32]{0:T(128)S(1)}, s32[32]{0:T(128)}, u32[]{:S(2)}) copy-start(s32[32]{0:T(128)} %param.13) | copy-start | bytes 388
  7.6 36.8 %copy-start.1 = (f32[8,1792]{1,0:T(8,128)S(1)}, f32[8,1792]{1,0:T(8,128)}, u32[]{:S(2)}) copy-start(f32[8,1792]{1,0:T(8,128)} %f_ref.3) | copy-start | bytes 172036
  7.6 36.8 %copy-start.2 = (f32[8,1792]{1,0:T(8,128)S(1)}, f32[8,1792]{1,0:T(8,128)}, u32[]{:S(2)}) copy-start(f32[8,1792]{1,0:T(8,128)} %s_ref.3) | copy-start | bytes 172036
  7.6 36.8 %copy-start.3 = (bf16[8,1792]{1,0:T(8,128)(2,1)S(1)}, bf16[8,1792]{1,0:T(8,128)(2,1)}, u32[]{:S(2)}) copy-start(bf16[8,1792]{1,0:T(8,128)(2,1)} %w_ref.3) | copy-start | bytes 86020
  8.6 35.7 %all-to-all-start.1 = ((f16[16,128,128]{2,1,0:T(8,128)(2,1)}), f16[16,128,128]{2,1,0:T(8,128)(2,1)S(1)}, u32[]{:S(2)}, u32[]{:S(2)}) async-start(f16[16,128,128]{2,1,0:T(8,128)(2,1)} %fusion.2), calls=%async_computation.1 | async-start | bytes 1048576 | tf_op jit(solution)/shard_map/all_to_all | solution.py:160
  46.3 40.3 %all-to-all-start.2 = ((f16[32,128,128]{2,1,0:T(8,128)(2,1)}), f16[32,128,128]{2,1,0:T(8,128)(2,1)S(1)}, u32[]{:S(2)}, u32[]{:S(2)}) async-start(f16[32,128,128]{2,1,0:T(8,128)(2,1)} %convert_element_type.29), calls=%async_computation.2 | async-start | bytes 2097152 | tf_op jit(solution)/shard_map/all_to_all | solution.py:171

commit v3 on v2

--- a/solution.py
+++ b/solution.py
@@ -57,7 +57,18 @@
     )(grads)
 
 
-def rows_kernel(scal, sums_ref, w_ref, f_ref, s_ref, out_ref, rows):
+def leaving_kernel(slot_ref, w_ref, f_ref, s_ref, out_ref, wide):
+    tiles = w_ref.shape[1] // LANES
+    wide[...] = w_ref[...].astype(F32)
+    out_ref[...] = jnp.zeros_like(out_ref)
+    is_slot = lax.broadcasted_iota(jnp.int32, wide.shape, 0) == slot_ref[0]
+    for n, ref in enumerate((wide, f_ref, s_ref)):
+        row = jnp.sum(jnp.where(is_slot, ref[...], 0.0), axis=0, keepdims=True) * STATE_SCALE
+        for t in range(tiles):
+            out_ref[n * tiles + t : n * tiles + t + 1, :] = row[:, t * LANES : (t + 1) * LANES]
+
+
+def rows_kernel(slot_ref, asked_ref, sums_ref, w_ref, f_ref, s_ref, out_ref, rows):
     homes, width = f_ref.shape
     tiles = width // LANES
     for n, ref in enumerate((w_ref, f_ref, s_ref)):
@@ -72,12 +83,15 @@
             at = 3 * tiles + t
             rows[i, at : at + 1, :] = sums[t * homes + i : t * homes + i + 1, :]
     extra = sums[tiles * homes :, :]
-    leaving = rows[scal[0]]
+    slot = slot_ref[0]
     per = 4 * tiles
+    rows[homes] = jnp.zeros_like(rows[homes])
+    rows[homes, :tiles, :] = rows[slot, 3 * tiles :, :]
+    leaving = rows[homes, :ROW, :]
     for d in range(out_ref.shape[0]):
-        out_ref[d, :per, :] = leaving
-        out_ref[d, per : 2 * per, :] = rows[scal[8 + d]]
-        out_ref[d, 2 * per :, :] = extra
+        out_ref[d, :per, :] = rows[asked_ref[d]]
+        out_ref[d, per : per + ROW, :] = extra
+        out_ref[d, per + ROW :, :] = leaving
 
 
 def adam(total, base, first, second):
@@ -87,20 +101,21 @@
     return base - 0.02 * (step + 0.1 * base), moment1, moment2
 
 
-def final_kernel(scal, sums_ref, extras_ref, got_ref, w_ref, f_ref, s_ref, nw_ref, nf_ref, ns_ref, acc, flat):
+def final_kernel(
+    slot_ref, adds_ref, extra_adds_ref, sums_ref, extras_ref, got_ref, w_ref, f_ref, s_ref, nw_ref, nf_ref, ns_ref, acc, flat
+):
     homes, width = f_ref.shape
     tiles = width // LANES
-    devices = extras_ref.shape[0]
-    slot = scal[0]
+    slot = slot_ref[0]
     acc[...] = jnp.zeros_like(acc)
-    for s in range(devices):
-        to = scal[8 + devices + s]
+    for s in range(extras_ref.shape[0]):
+        to = adds_ref[s]
 
         @pl.when(to >= 0)
         def _():
             acc[to] += extras_ref[s]
 
-        @pl.when(scal[8 + 2 * devices + s] > 0)
+        @pl.when(extra_adds_ref[s] > 0)
         def _():
             acc[homes] += extras_ref[s]
 
@@ -144,8 +159,25 @@
     asked = jnp.sum(jnp.where(new_extra[:, None] == my_old[None, :], ids[None, :], 0), axis=1)
     adds = jnp.sum(jnp.where(old_extra[:, None] == my_new[None, :], ids[None, :] + 1, 0), axis=1) - 1
     extra_adds = (old_extra == wanted).astype(jnp.int32)
-    head = jnp.stack([slot, source, extra_source] + [slot] * 5)
-    return jnp.concatenate([head, asked, adds, extra_adds])
+    return slot, source, extra_source, asked, adds, extra_adds
+
+
+def gather_leaving(row):
+    devices = lax.axis_size("expert")
+    me = lax.axis_index("expert")
+    bits = [1 << k for k in range(devices.bit_length() - 1)]
+    if len(bits) == 5:
+        bits = [bits[k] for k in (4, 3, 1, 0, 2)]
+    held = row[None]
+    for bit in bits:
+        other = lax.ppermute(held, "expert", [(i, i ^ bit) for i in range(devices)])
+        held = jnp.concatenate([held, other], axis=0)
+
+    def place(source):
+        apart = jnp.bitwise_xor(source, me)
+        return sum(jnp.where(jnp.bitwise_and(apart, bit) != 0, 1 << k, 0) for k, bit in enumerate(bits))
+
+    return held, place
 
 
 def per_device(grads, weights, first, second, old_home, old_extra, new_home, new_extra):
@@ -153,7 +185,18 @@
     tiles = width // LANES
     outer = lax.axis_size("outer")
     devices = lax.axis_size("expert")
-    scal = routes(homes, old_home, old_extra, new_home, new_extra)
+    slot, source, extra_source, asked, adds, extra_adds = routes(homes, old_home, old_extra, new_home, new_extra)
+    slot = slot.reshape(1)
+    leaving = pl.pallas_call(
+        leaving_kernel,
+        in_specs=[SMEM] + [VMEM] * 3,
+        out_specs=VMEM,
+        out_shape=jax.ShapeDtypeStruct((3 * ROW, LANES), F32),
+        scratch_shapes=[pltpu.VMEM((homes, width), F32)],
+        compiler_params=pltpu.CompilerParams(vmem_limit_bytes=16 * 2**20),
+        cost_estimate=cost(1 << 16),
+    )(slot, weights, first, second)
+    held, place = gather_leaving(leaving.astype(F16))
     halves = split_by_core(grads, outer, width)
     pair = lax.all_to_all(halves, "core", 0, 0, tiled=True).astype(F32)
     partial = ((pair[0] + pair[1]) * PAIR_SCALE).astype(F16)
@@ -161,21 +204,22 @@
     sums = jnp.sum(parts.astype(F32), axis=0) * (1.0 / PAIR_SCALE)
     outgoing = pl.pallas_call(
         rows_kernel,
-        in_specs=[SMEM] + [VMEM] * 4,
+        in_specs=[SMEM] * 2 + [VMEM] * 4,
         out_specs=VMEM,
-        out_shape=jax.ShapeDtypeStruct((devices, 8 * tiles + ROW, LANES), F32),
-        scratch_shapes=[pltpu.VMEM((homes, 4 * tiles, LANES), F32)],
+        out_shape=jax.ShapeDtypeStruct((devices, 4 * tiles + 2 * ROW, LANES), F32),
+        scratch_shapes=[pltpu.VMEM((homes + 1, 4 * tiles, LANES), F32)],
         compiler_params=pltpu.CompilerParams(vmem_limit_bytes=16 * 2**20),
         cost_estimate=cost(1 << 18),
-    )(scal, sums, weights, first, second)
+    )(slot, asked, sums, weights, first, second)
     arrived = lax.all_to_all(outgoing.astype(F16), "expert", 0, 0, tiled=True)
-    extras = arrived[:, 8 * tiles :, :].astype(F32)
-    moved = lax.dynamic_slice(arrived, (scal[1], 0, 0), (1, 4 * tiles, LANES))
-    copied = lax.dynamic_slice(arrived, (scal[2], 4 * tiles, 0), (1, 4 * tiles, LANES))
-    got = jnp.concatenate([moved[0], copied[0]], axis=0).astype(F32)
+    extras = arrived[:, 4 * tiles : 4 * tiles + ROW, :].astype(F32)
+    state = lax.dynamic_index_in_dim(held, place(source), 0, keepdims=False)[: 3 * tiles]
+    moved = lax.dynamic_slice(arrived, (source, 4 * tiles + ROW, 0), (1, tiles, LANES))
+    copied = lax.dynamic_slice(arrived, (extra_source, 0, 0), (1, 4 * tiles, LANES))
+    got = jnp.concatenate([state, moved[0], copied[0]], axis=0).astype(F32)
     return pl.pallas_call(
         final_kernel,
-        in_specs=[SMEM] + [VMEM] * 6,
+        in_specs=[SMEM] * 3 + [VMEM] * 6,
         out_specs=[VMEM] * 3,
         out_shape=[
             jax.ShapeDtypeStruct((homes + 1, width), BF16),
@@ -185,7 +229,7 @@
         scratch_shapes=[pltpu.VMEM((homes + 1, ROW, LANES), F32), pltpu.VMEM((3 * homes, width), F32)],
         compiler_params=pltpu.CompilerParams(vmem_limit_bytes=16 * 2**20),
         cost_estimate=cost(1 << 18),
-    )(scal, sums, extras, got, weights, first, second)
+    )(slot, adds, extra_adds, sums, extras, got, weights, first, second)
 
 
 def solution(mesh):

time: 89.9 us -> 105 us (1.17)
  starting transfers between devices: 30.3 us -> 62.3 us
  waiting for transfers between devices: 32.5 us -> 18.1 us
  local copies, waits for them, and re-layouts: 7.35 us -> 2.35 us
  Pallas kernels: 3.26 us -> 5.16 us
    ppermute x0 -> x5, starting transfers between devices: none -> 32 us  [gather_leaving(): other = lax.ppermute(held, 'expert', [(i, i ^ bit) for i in range(devices)])]
    all_to_all x1, waiting for transfers between devices: 22.6 us -> 0.01 us  [per_device(): arrived = lax.all_to_all(outgoing.astype(F16), 'expert', 0, 0, tiled=True)]
    ppermute x0 -> x5, waiting for transfers between devices: none -> 12.7 us  [gather_leaving(): other = lax.ppermute(held, 'expert', [(i, i ^ bit) for i in range(devices)])]
    concatenate x1 -> x2, local copies, waits for them, and re-layouts: 5.2 us -> 0.11 us  [gather_leaving(): held = jnp.concatenate([held, other], axis=0)]
    all_to_all x1, waiting for transfers between devices: 9.92 us -> 5.43 us  [per_device(): parts = lax.all_to_all(partial, 'outer', 0, 0, tiled=True)]
    pallas_call x2 -> x3, Pallas kernels: 2.68 us -> 4.58 us  [the longest x1 2.56 us: per_device(): pl.pallas_call(final_kernel, in_specs=[SMEM] * 3 + [VMEM] * 6, out_specs=...]
  transfers between devices with their start and end apart: 2 -> 7, of which waited for: 2 -> 5; matrix products, arithmetic and copies ran while one was open for 11% -> 5% of each run, Pallas kernels for 0% -> 2%
where the time goes in v3:
time: 105 us; the launch traced here: 104 us
  starting transfers between devices  62.3 us (59%)
  waiting for transfers between devices  18.1 us (17%)
  other arithmetic  5.85 us (6%)
  between operations  5.17 us (5%)
  Pallas kernels  5.16 us (5%)
  blocking collectives  4.58 us (4%)
  local copies, waits for them, and re-layouts  2.35 us (2%)
    ppermute x5, starting transfers between devices, gather_leaving(): other = lax.ppermute(held, 'expert', [(i, i ^ bit) for i in range(devices)])  32 us
    all_to_all x1, starting transfers between devices, per_device(): parts = lax.all_to_all(partial, 'outer', 0, 0, tiled=True)  16.4 us
    all_to_all x1, starting transfers between devices, per_device(): arrived = lax.all_to_all(outgoing.astype(F16), 'expert', 0, 0, tiled=True)  13.9 us
    ppermute x5, waiting for transfers between devices, gather_leaving(): other = lax.ppermute(held, 'expert', [(i, i ^ bit) for i in range(devices)])  12.7 us
    all_to_all x1, waiting for transfers between devices, per_device(): parts = lax.all_to_all(partial, 'outer', 0, 0, tiled=True)  5.43 us
    all_to_all x1, blocking collectives, per_device(): pair = lax.all_to_all(halves, 'core', 0, 0, tiled=True).astype(F32)  4.58 us
    pallas_call x1, Pallas kernels, per_device(): pl.pallas_call(final_kernel, in_specs=[SMEM] * 3 + [VMEM] * 6, out_specs=...  2.56 us
  transfers between devices with their start and end apart: 7, of which 5 were waited for; matrix products, arithmetic and copies ran while one was open for 5% of the time, Pallas kernels for 2%

profile of v3, /device:TPU:14, one launch (start us, length us, event | category | flops | bytes accessed | tf_op | source)
XLA Modules:
  0.0 103.5 jit_solution(6591090702718915818)
XLA Ops:
  0.6 0.0 copy-start
  0.6 1.5 %copy-done = bf16[1,9,57344]{2,1,0:T(8,128)(2,1)S(1)} copy-done((bf16[1,9,57344]{2,1,0:T(8,128)(2,1)S(1)}, bf16[1,9,57344]{2,1,0:T(8,128)(2,1)}, u32[]{:S(2)}) %copy-start) | copy-done | bytes 1032216
  2.1 0.6 shard_map.103
  2.7 4.6 %all_to_all.15 = bf16[2,16,128,128]{3,2,1,0:T(8,128)(2,1)S(1)} all-to-all(bf16[2,16,128,128]{3,2,1,0:T(8,128)(2,1)S(1)} %shard_map.103), channel_id=1, replica_groups=mesh['outer'=16,'core'=2,'expert'=32] {'core'}, dimensions={0} | all-to-all | bytes 2097152 | tf_op jit(solution)/shard_map/all_to_all | solution.py:201
  7.3 0.2 convert_element_type.28
  7.5 0.0 copy-start.4
  7.5 0.0 copy-start.6
  7.6 0.0 copy-start.1
  7.6 0.0 copy-start.2
  7.6 0.0 copy-start.3
  7.6 0.0 copy-start.7
  7.6 0.0 copy-start.5
  7.6 1.0 fusion.2
  8.6 16.4 %all-to-all-start.1 = ((f16[16,128,128]{2,1,0:T(8,128)(2,1)}), f16[16,128,128]{2,1,0:T(8,128)(2,1)S(1)}, u32[]{:S(2)}, u32[]{:S(2)}) async-start(f16[16,128,128]{2,1,0:T(8,128)(2,1)} %fusion.2), calls=%async_computation.1 | async-start | bytes 1048576 | tf_op jit(solution)/shard_map/all_to_all | solution.py:203
  25.0 0.0 copy-done.4
  25.0 0.0 copy-done.6
  25.0 0.8 fusion.6
  25.8 0.0 copy-done.1
  25.8 0.0 copy-done.2
  25.8 0.0 copy-done.3
  25.8 0.7 shard_map.105
  26.5 11.0 %collective-permute-start = (f16[1,48,128]{2,1,0:T(8,128)(2,1)S(1)}, f16[1,48,128]{2,1,0:T(8,128)(2,1)S(1)}, u32[]{:S(2)}, u32[]{:S(2)}) collective-permute-start(f16[1,48,128]{2,1,0:T(8,128)(2,1)S(1)} %get-tuple-element.8), channel_id=1, source_target_pairs={{0,16},{1,17},{2,18},{3,19},{4,20},{5,21},{6,22},{7,23},{8,24},{9,... | collective-permute-start | bytes 36872 | tf_op jit(solution)/shard_map/ppermute | solution.py:173
  37.5 0.0 copy-done.7
  37.5 0.6 dynamic_slice.21
  38.1 0.1 select_reduce_fusion.asked_ref
  38.2 0.0 copy-done.5
  38.2 0.6 compare_convert_fusion.extra_adds_ref
  38.8 5.4 %all-to-all-done.1 = f16[16,128,128]{2,1,0:T(8,128)(2,1)S(1)} async-done(((f16[16,128,128]{2,1,0:T(8,128)(2,1)}), f16[16,128,128]{2,1,0:T(8,128)(2,1)S(1)}, u32[]{:S(2)}, u32[]{:S(2)}) %all-to-all-start.1) | async-done | bytes 524320 | tf_op jit(solution)/shard_map/all_to_all | solution.py:203
  44.3 0.1 convert_reduce_fusion
  44.4 0.1 select_reduce_fusion.1
  44.4 1.3 %shard_map.104 = f32[32,88,128]{2,1,0:T(8,128)S(1)} custom-call(s32[1]{0:T(128)} %bitcast.slot_ref, s32[32]{0:T(128)S(1)} %select_reduce_fusion.asked_ref, f32[128,128]{1,0:T(8,128)S(1)} %broadcast_multiply_fusion.sums_ref, bf16[8,1792]{1,0:T(8,128)(2,1)S(1)} %copy-done.3, f32[8,1792]{1,0:T(8,128)S(1)} %copy-done.1, f32[8,1792]{1,0:T(8,128)S(1)} %copy-done.2), custom_call_target="tpu_custom_call" | custom-call | flops 262144 | bytes 1048576 | tf_op jit(solution)/shard_map/pallas_call | solution.py:205
  45.8 1.0 convert_element_type.32
  46.7 13.9 %all-to-all-start.2 = ((f16[32,88,128]{2,1,0:T(8,128)(2,1)}), f16[32,88,128]{2,1,0:T(8,128)(2,1)S(1)}, u32[]{:S(2)}, u32[]{:S(2)}) async-start(f16[32,88,128]{2,1,0:T(8,128)(2,1)} %convert_element_type.32), calls=%async_computation.2 | async-start | bytes 1441792 | tf_op jit(solution)/shard_map/all_to_all | solution.py:214
  60.7 1.9 %fusion.3 = (s32[]{:T(128)}, s32[]{:T(128)}) fusion(s32[256]{0:T(256)S(1)} %copy-done.4, s32[]{:T(128)} %get-tuple-element.5, s32[]{:T(128)} %bitcast.1), kind=kLoop, calls=%fused_computation.37 | loop fusion | flops 3582 | bytes 1040 | tf_op jit(solution)/shard_map/reduce_sum | solution.py:157
  66.9 0.0 collective-permute-done
  66.9 4.6 %collective-permute-start.1 = (f16[2,48,128]{2,1,0:T(8,128)(2,1)S(1)}, f16[2,48,128]{2,1,0:T(8,128)(2,1)S(1)}, u32[]{:S(2)}, u32[]{:S(2)}) collective-permute-start(f16[2,48,128]{2,1,0:T(8,128)(2,1)S(1)} %pad_maximum_fusion.2), channel_id=1, source_target_pairs={{0,8},{1,9},{2,10},{3,11},{4,12},{5,13},{6,14},{7,15},{8,0},{9,1},... | collective-permute-start | bytes 73736 | tf_op jit(solution)/shard_map/ppermute | solution.py:173
  71.5 4.5 %collective-permute-done.1 = f16[2,48,128]{2,1,0:T(8,128)(2,1)S(1)} collective-permute-done((f16[2,48,128]{2,1,0:T(8,128)(2,1)S(1)}, f16[2,48,128]{2,1,0:T(8,128)(2,1)S(1)}, u32[]{:S(2)}, u32[]{:S(2)}) %collective-permute-start.1) | collective-permute-done | bytes 24608 | tf_op jit(solution)/shard_map/ppermute | solution.py:173
  76.0 7.8 %collective-permute-start.2 = (f16[4,48,128]{2,1,0:T(8,128)(2,1)S(1)}, f16[4,48,128]{2,1,0:T(8,128)(2,1)S(1)}, u32[]{:S(2)}, u32[]{:S(2)}) collective-permute-start(f16[4,48,128]{2,1,0:T(8,128)(2,1)S(1)} %pad_maximum_fusion.1), channel_id=1, source_target_pairs={{0,2},{1,3},{2,0},{3,1},{4,6},{5,7},{6,4},{7,5},{8,10},{9,11},{10,... | collective-permute-start | bytes 147464 | tf_op jit(solution)/shard_map/ppermute | solution.py:173
  83.8 2.0 %collective-permute-done.2 = f16[4,48,128]{2,1,0:T(8,128)(2,1)S(1)} collective-permute-done((f16[4,48,128]{2,1,0:T(8,128)(2,1)S(1)}, f16[4,48,128]{2,1,0:T(8,128)(2,1)S(1)}, u32[]{:S(2)}, u32[]{:S(2)}) %collective-permute-start.2) | collective-permute-done | bytes 49184 | tf_op jit(solution)/shard_map/ppermute | solution.py:173
  85.9 4.4 %collective-permute-start.3 = (f16[8,48,128]{2,1,0:T(8,128)(2,1)S(1)}, f16[8,48,128]{2,1,0:T(8,128)(2,1)S(1)}, u32[]{:S(2)}, u32[]{:S(2)}) collective-permute-start(f16[8,48,128]{2,1,0:T(8,128)(2,1)S(1)} %pad_maximum_fusion), channel_id=1, source_target_pairs={{0,1},{1,0},{2,3},{3,2},{4,5},{5,4},{6,7},{7,6},{8,9},{9,8},{10,11... | collective-permute-start | bytes 294920 | tf_op jit(solution)/shard_map/ppermute | solution.py:173
  90.3 2.5 %collective-permute-done.3 = f16[8,48,128]{2,1,0:T(8,128)(2,1)S(1)} collective-permute-done((f16[8,48,128]{2,1,0:T(8,128)(2,1)S(1)}, f16[8,48,128]{2,1,0:T(8,128)(2,1)S(1)}, u32[]{:S(2)}, u32[]{:S(2)}) %collective-permute-start.3) | collective-permute-done | bytes 98336 | tf_op jit(solution)/shard_map/ppermute | solution.py:173
  92.9 0.1 constant_dynamic-update-slice_fusion
  92.9 4.2 %collective-permute-start.4 = (f16[16,48,128]{2,1,0:T(8,128)(2,1)S(1)}, f16[16,48,128]{2,1,0:T(8,128)(2,1)S(1)}, u32[]{:S(2)}, u32[]{:S(2)}) collective-permute-start(f16[16,48,128]{2,1,0:T(8,128)(2,1)S(1)} %get-tuple-element.11), channel_id=1, source_target_pairs={{0,4},{1,5},{2,6},{3,7},{4,0},{5,1},{6,2},{7,3},{8,12},{9,13},{10,... | collective-permute-start | bytes 589832 | tf_op jit(solution)/shard_map/ppermute | solution.py:173
  97.2 3.6 %collective-permute-done.4 = f16[16,48,128]{2,1,0:T(8,128)(2,1)S(1)} collective-permute-done((f16[16,48,128]{2,1,0:T(8,128)(2,1)S(1)}, f16[16,48,128]{2,1,0:T(8,128)(2,1)S(1)}, u32[]{:S(2)}, u32[]{:S(2)}) %collective-permute-start.4) | collective-permute-done | bytes 196640 | tf_op jit(solution)/shard_map/ppermute | solution.py:173
  100.8 0.1 constant_dynamic-update-slice_fusion.5
  100.9 0.0 all-to-all-done.2
  101.0 2.6 %shard_map.106 = (bf16[9,1792]{1,0:T(8,128)(2,1)}, f32[8,1792]{1,0:T(8,128)}, f32[8,1792]{1,0:T(8,128)}) custom-call(s32[1]{0:T(128)} %bitcast.slot_ref, s32[32]{0:T(128)S(1)} %broadcast_add_fusion.adds_ref, s32[32]{0:T(128)S(1)} %compare_convert_fusion.extra_adds_ref, f32[128,128]{1,0:T(8,128)S(1)} %broadcast_multiply_fusion.sums_ref, ...), custom_call_target="tpu_custom_call" | custom-call | flops 262144 | bytes 1048576 | tf_op jit(solution)/shard_map/pallas_call | solution.py:220
  (15 shorter events, 0.2 us)
Async XLA Ops:
  0.6 1.5 %copy-start = (bf16[1,9,57344]{2,1,0:T(8,128)(2,1)S(1)}, bf16[1,9,57344]{2,1,0:T(8,128)(2,1)}, u32[]{:S(2)}) copy-start(bf16[1,9,57344]{2,1,0:T(8,128)(2,1)} %refs_0_.1) | copy-start | bytes 3096580
  7.5 17.5 %copy-start.4 = (s32[256]{0:T(256)S(1)}, s32[256]{0:T(256)}, u32[]{:S(2)}) copy-start(s32[256]{0:T(256)} %param.12) | copy-start | bytes 3076
  7.5 17.4 %copy-start.6 = (s32[256]{0:T(256)S(1)}, s32[256]{0:T(256)}, u32[]{:S(2)}) copy-start(s32[256]{0:T(256)} %param.14) | copy-start | bytes 3076
  7.6 18.2 %copy-start.1 = (f32[8,1792]{1,0:T(8,128)S(1)}, f32[8,1792]{1,0:T(8,128)}, u32[]{:S(2)}) copy-start(f32[8,1792]{1,0:T(8,128)} %f_ref.5) | copy-start | bytes 172036
  7.6 18.2 %copy-start.2 = (f32[8,1792]{1,0:T(8,128)S(1)}, f32[8,1792]{1,0:T(8,128)}, u32[]{:S(2)}) copy-start(f32[8,1792]{1,0:T(8,128)} %s_ref.5) | copy-start | bytes 172036
  7.6 18.2 %copy-start.3 = (bf16[8,1792]{1,0:T(8,128)(2,1)S(1)}, bf16[8,1792]{1,0:T(8,128)(2,1)}, u32[]{:S(2)}) copy-start(bf16[8,1792]{1,0:T(8,128)(2,1)} %w_ref.5) | copy-start | bytes 86020
  7.6 29.9 %copy-start.7 = (s32[32]{0:T(128)S(1)}, s32[32]{0:T(128)}, u32[]{:S(2)}) copy-start(s32[32]{0:T(128)} %param.15) | copy-start | bytes 388
  7.6 30.6 %copy-start.5 = (s32[32]{0:T(128)S(1)}, s32[32]{0:T(128)}, u32[]{:S(2)}) copy-start(s32[32]{0:T(128)} %param.13) | copy-start | bytes 388
  8.6 35.7 %all-to-all-start.1 = ((f16[16,128,128]{2,1,0:T(8,128)(2,1)}), f16[16,128,128]{2,1,0:T(8,128)(2,1)S(1)}, u32[]{:S(2)}, u32[]{:S(2)}) async-start(f16[16,128,128]{2,1,0:T(8,128)(2,1)} %fusion.2), calls=%async_computation.1 | async-start | bytes 1048576 | tf_op jit(solution)/shard_map/all_to_all | solution.py:203
  26.5 40.4 %collective-permute-start = (f16[1,48,128]{2,1,0:T(8,128)(2,1)S(1)}, f16[1,48,128]{2,1,0:T(8,128)(2,1)S(1)}, u32[]{:S(2)}, u32[]{:S(2)}) collective-permute-start(f16[1,48,128]{2,1,0:T(8,128)(2,1)S(1)} %get-tuple-element.8), channel_id=1, source_target_pairs={{0,16},{1,17},{2,18},{3,19},{4,20},{5,21},{6,22},{7,23},{8,24},{9,... | collective-permute-start | bytes 36872 | tf_op jit(solution)/shard_map/ppermute | solution.py:173
  46.7 54.1 %all-to-all-start.2 = ((f16[32,88,128]{2,1,0:T(8,128)(2,1)}), f16[32,88,128]{2,1,0:T(8,128)(2,1)S(1)}, u32[]{:S(2)}, u32[]{:S(2)}) async-start(f16[32,88,128]{2,1,0:T(8,128)(2,1)} %convert_element_type.32), calls=%async_computation.2 | async-start | bytes 1441792 | tf_op jit(solution)/shard_map/all_to_all | solution.py:214
  66.9 9.1 %collective-permute-start.1 = (f16[2,48,128]{2,1,0:T(8,128)(2,1)S(1)}, f16[2,48,128]{2,1,0:T(8,128)(2,1)S(1)}, u32[]{:S(2)}, u32[]{:S(2)}) collective-permute-start(f16[2,48,128]{2,1,0:T(8,128)(2,1)S(1)} %pad_maximum_fusion.2), channel_id=1, source_target_pairs={{0,8},{1,9},{2,10},{3,11},{4,12},{5,13},{6,14},{7,15},{8,0},{9,1},... | collective-permute-start | bytes 73736 | tf_op jit(solution)/shard_map/ppermute | solution.py:173
  76.0 9.8 %collective-permute-start.2 = (f16[4,48,128]{2,1,0:T(8,128)(2,1)S(1)}, f16[4,48,128]{2,1,0:T(8,128)(2,1)S(1)}, u32[]{:S(2)}, u32[]{:S(2)}) collective-permute-start(f16[4,48,128]{2,1,0:T(8,128)(2,1)S(1)} %pad_maximum_fusion.1), channel_id=1, source_target_pairs={{0,2},{1,3},{2,0},{3,1},{4,6},{5,7},{6,4},{7,5},{8,10},{9,11},{10,... | collective-permute-start | bytes 147464 | tf_op jit(solution)/shard_map/ppermute | solution.py:173
  85.9 7.0 %collective-permute-start.3 = (f16[8,48,128]{2,1,0:T(8,128)(2,1)S(1)}, f16[8,48,128]{2,1,0:T(8,128)(2,1)S(1)}, u32[]{:S(2)}, u32[]{:S(2)}) collective-permute-start(f16[8,48,128]{2,1,0:T(8,128)(2,1)S(1)} %pad_maximum_fusion), channel_id=1, source_target_pairs={{0,1},{1,0},{2,3},{3,2},{4,5},{5,4},{6,7},{7,6},{8,9},{9,8},{10,11... | collective-permute-start | bytes 294920 | tf_op jit(solution)/shard_map/ppermute | solution.py:173
  92.9 7.9 %collective-permute-start.4 = (f16[16,48,128]{2,1,0:T(8,128)(2,1)S(1)}, f16[16,48,128]{2,1,0:T(8,128)(2,1)S(1)}, u32[]{:S(2)}, u32[]{:S(2)}) collective-permute-start(f16[16,48,128]{2,1,0:T(8,128)(2,1)S(1)} %get-tuple-element.11), channel_id=1, source_target_pairs={{0,4},{1,5},{2,6},{3,7},{4,0},{5,1},{6,2},{7,3},{8,12},{9,13},{10,... | collective-permute-start | bytes 589832 | tf_op jit(solution)/shard_map/ppermute | solution.py:173

commit v4 on v2

--- a/solution.py
+++ b/solution.py
@@ -9,6 +9,8 @@
 bias_first = 0.9999734386011124
 bias_second = 0.994079470779696
 LANES = 128
+PLANE = 4
+ORDER = (0, 2, 1, 3)
 ROW = 16
 PAIR_SCALE = 4096.0
 SUM_SCALE = 256.0
@@ -57,27 +59,46 @@
     )(grads)
 
 
-def rows_kernel(scal, sums_ref, w_ref, f_ref, s_ref, out_ref, rows):
-    homes, width = f_ref.shape
-    tiles = width // LANES
-    for n, ref in enumerate((w_ref, f_ref, s_ref)):
-        value = ref[...].astype(F32) * STATE_SCALE
-        for i in range(homes):
-            for t in range(tiles):
-                at = n * tiles + t
-                rows[i, at : at + 1, :] = value[i : i + 1, t * LANES : (t + 1) * LANES]
+def starts(tiles):
+    per = -(-tiles // PLANE)
+    return per, [min(y * per, tiles - per) for y in range(PLANE)]
+
+
+def rows_kernel(slot_ref, mine_ref, asked_ref, moves_ref, wants_ref, sums_ref, held_ref, out_ref, state_a, state_b, sent):
+    homes = sent.shape[0]
+    tiles = held_ref.shape[3] // LANES
+    per, _ = starts(tiles)
+    mine = mine_ref[0]
+    first_tile = jnp.minimum(mine * per, tiles - per)
+    state_a[...] = jnp.zeros_like(state_a)
+    state_b[...] = jnp.zeros_like(state_b)
+    for r in range(PLANE):
+        base = jnp.bitwise_xor(mine, ORDER[r]) * homes
+        for n in range(3):
+            for k in range(per):
+                at = pl.multiple_of((first_tile + k) * LANES, LANES)
+                value = held_ref[r, n, :, pl.ds(at, LANES)]
+                for i in range(homes):
+                    state_a[base + i, n * per + k : n * per + k + 1, :] = value[i : i + 1, :]
+                    state_b[base + i, (3 + n) * per + k : (3 + n) * per + k + 1, :] = value[i : i + 1, :]
     sums = sums_ref[...] * SUM_SCALE
+    slot = slot_ref[0]
+    sent[...] = jnp.zeros_like(sent)
     for i in range(homes):
         for t in range(tiles):
-            at = 3 * tiles + t
-            rows[i, at : at + 1, :] = sums[t * homes + i : t * homes + i + 1, :]
-    extra = sums[tiles * homes :, :]
-    leaving = rows[scal[0]]
-    per = 4 * tiles
+            sent[i, tiles + t : tiles + t + 1, :] = sums[t * homes + i : t * homes + i + 1, :]
+    leaving = sent[slot]
+    for t in range(tiles):
+        at = tiles * homes + t
+        for i in range(homes):
+            row = 2 * tiles + t
+            sent[i, row : row + 1, :] = sent[i, tiles + t : tiles + t + 1, :]
+            sent[i, tiles + t : tiles + t + 1, :] = leaving[tiles + t : tiles + t + 1, :]
+            sent[i, t : t + 1, :] = sums[at : at + 1, :]
+    head = 6 * per
     for d in range(out_ref.shape[0]):
-        out_ref[d, :per, :] = leaving
-        out_ref[d, per : 2 * per, :] = rows[scal[8 + d]]
-        out_ref[d, 2 * per :, :] = extra
+        out_ref[d, :head, :] = state_a[moves_ref[d]] + state_b[wants_ref[d]]
+        out_ref[d, head:, :] = sent[asked_ref[d]]
 
 
 def adam(total, base, first, second):
@@ -87,30 +108,41 @@
     return base - 0.02 * (step + 0.1 * base), moment1, moment2
 
 
-def final_kernel(scal, sums_ref, extras_ref, got_ref, w_ref, f_ref, s_ref, nw_ref, nf_ref, ns_ref, acc, flat):
+def final_kernel(
+    slot_ref, adds_ref, extra_adds_ref, sums_ref, extras_ref, states_ref, totals_ref, w_ref, f_ref, s_ref, nw_ref, nf_ref, ns_ref, acc, flat
+):
     homes, width = f_ref.shape
     tiles = width // LANES
-    devices = extras_ref.shape[0]
-    slot = scal[0]
+    per, firsts = starts(tiles)
+    slot = slot_ref[0]
     acc[...] = jnp.zeros_like(acc)
-    for s in range(devices):
-        to = scal[8 + devices + s]
+    for s in range(extras_ref.shape[0]):
+        to = adds_ref[s]
 
         @pl.when(to >= 0)
         def _():
             acc[to] += extras_ref[s]
 
-        @pl.when(scal[8 + 2 * devices + s] > 0)
+        @pl.when(extra_adds_ref[s] > 0)
         def _():
             acc[homes] += extras_ref[s]
 
+    for y in range(PLANE):
+        for k in range(per):
+            cols = slice((firsts[y] + k) * LANES, (firsts[y] + k + 1) * LANES)
+            for h in range(2):
+                for n in range(3):
+                    to = 2 * homes + 4 * h + n
+                    at = (3 * h + n) * per + k
+                    flat[to : to + 1, cols] = states_ref[h, y, at : at + 1, :]
     for t in range(tiles):
         cols = slice(t * LANES, (t + 1) * LANES)
         for i in range(homes + 1):
             flat[i : i + 1, cols] = acc[i, t : t + 1, :]
-        for n in range(8):
-            at = n * tiles + t
-            flat[2 * homes + n : 2 * homes + n + 1, cols] = got_ref[at : at + 1, :]
+        for h in range(2):
+            to = 2 * homes + 4 * h + 3
+            at = (h + 1) * tiles + t
+            flat[to : to + 1, cols] = totals_ref[h, at : at + 1, :]
     is_new = lax.broadcasted_iota(jnp.int32, (homes, LANES), 0) == slot
     for t in range(tiles):
         cols = slice(t * LANES, (t + 1) * LANES)
@@ -131,21 +163,34 @@
 
 def routes(homes, old_home, old_extra, new_home, new_extra):
     me = lax.axis_index("expert")
+    my_new = lax.dynamic_slice_in_dim(new_home, me * homes, homes)
     my_old = lax.dynamic_slice_in_dim(old_home, me * homes, homes)
-    my_new = lax.dynamic_slice_in_dim(new_home, me * homes, homes)
     wanted = lax.dynamic_slice_in_dim(new_extra, me, 1)
     ids = jnp.arange(homes, dtype=jnp.int32)
-    changed = my_old != my_new
-    slot = jnp.sum(jnp.where(changed, ids, 0))
-    arriving = jnp.sum(jnp.where(changed, my_new, 0))
-    owner = jnp.arange(old_home.shape[0], dtype=jnp.int32) // homes
-    source = jnp.sum(jnp.where(old_home == arriving, owner, 0))
-    extra_source = jnp.sum(jnp.where(old_home == wanted, owner, 0))
-    asked = jnp.sum(jnp.where(new_extra[:, None] == my_old[None, :], ids[None, :], 0), axis=1)
+    slot = jnp.sum(jnp.where(my_old != my_new, ids, 0)).reshape(1)
+    places = jnp.arange(old_home.shape[0], dtype=jnp.int32)
+    device = jnp.arange(new_extra.shape[0], dtype=jnp.int32)
+    arrives = (old_home != new_home)[None, :] & (places[None, :] // homes == device[:, None])
+    arriving = jnp.sum(jnp.where(arrives, new_home[None, :], 0), axis=1)
+    moves = jnp.sum(jnp.where(arriving[:, None] == old_home[None, :], places[None, :], 0), axis=1)
+    wants = jnp.sum(jnp.where(new_extra[:, None] == old_home[None, :], places[None, :], 0), axis=1)
+    source = jnp.sum(jnp.where(device == me, moves // homes, 0))
+    extra_source = jnp.sum(jnp.where(device == me, wants // homes, 0))
+    asked = jnp.where(wants // homes == me, wants % homes, 0)
     adds = jnp.sum(jnp.where(old_extra[:, None] == my_new[None, :], ids[None, :] + 1, 0), axis=1) - 1
     extra_adds = (old_extra == wanted).astype(jnp.int32)
-    head = jnp.stack([slot, source, extra_source] + [slot] * 5)
-    return jnp.concatenate([head, asked, adds, extra_adds])
+    plane = PLANE * homes
+    return slot, source, extra_source, asked, moves % plane, wants % plane, adds, extra_adds
+
+
+def share_states(weights, first, second):
+    devices = lax.axis_size("expert")
+    states = jnp.stack([weights.astype(F32), first, second])
+    held = (states * STATE_SCALE).astype(F16)[None]
+    for bit in (2, 1):
+        other = lax.ppermute(held, "expert", [(i, i ^ bit) for i in range(devices)])
+        held = jnp.concatenate([held, other], axis=0)
+    return held.astype(F32)
 
 
 def per_device(grads, weights, first, second, old_home, old_extra, new_home, new_extra):
@@ -153,29 +198,41 @@
     tiles = width // LANES
     outer = lax.axis_size("outer")
     devices = lax.axis_size("expert")
-    scal = routes(homes, old_home, old_extra, new_home, new_extra)
+    tables = routes(homes, old_home, old_extra, new_home, new_extra)
+    slot, source, extra_source, asked, moves, wants, adds, extra_adds = tables
+    held = share_states(weights, first, second)
+    mine = (lax.axis_index("expert") % PLANE).astype(jnp.int32).reshape(1)
     halves = split_by_core(grads, outer, width)
     pair = lax.all_to_all(halves, "core", 0, 0, tiled=True).astype(F32)
     partial = ((pair[0] + pair[1]) * PAIR_SCALE).astype(F16)
     parts = lax.all_to_all(partial, "outer", 0, 0, tiled=True)
     sums = jnp.sum(parts.astype(F32), axis=0) * (1.0 / PAIR_SCALE)
+    per, _ = starts(tiles)
+    head = 6 * per
+    tail = -(-3 * tiles // 8) * 8
     outgoing = pl.pallas_call(
         rows_kernel,
-        in_specs=[SMEM] + [VMEM] * 4,
+        in_specs=[SMEM] * 5 + [VMEM] * 2,
         out_specs=VMEM,
-        out_shape=jax.ShapeDtypeStruct((devices, 8 * tiles + ROW, LANES), F32),
-        scratch_shapes=[pltpu.VMEM((homes, 4 * tiles, LANES), F32)],
+        out_shape=jax.ShapeDtypeStruct((devices, head + tail, LANES), F32),
+        scratch_shapes=[
+            pltpu.VMEM((PLANE * homes, head, LANES), F32),
+            pltpu.VMEM((PLANE * homes, head, LANES), F32),
+            pltpu.VMEM((homes, tail, LANES), F32),
+        ],
         compiler_params=pltpu.CompilerParams(vmem_limit_bytes=16 * 2**20),
         cost_estimate=cost(1 << 18),
-    )(scal, sums, weights, first, second)
+    )(slot, mine, asked, moves, wants, sums, held)
     arrived = lax.all_to_all(outgoing.astype(F16), "expert", 0, 0, tiled=True)
-    extras = arrived[:, 8 * tiles :, :].astype(F32)
-    moved = lax.dynamic_slice(arrived, (scal[1], 0, 0), (1, 4 * tiles, LANES))
-    copied = lax.dynamic_slice(arrived, (scal[2], 4 * tiles, 0), (1, 4 * tiles, LANES))
-    got = jnp.concatenate([moved[0], copied[0]], axis=0).astype(F32)
+    extras = arrived[:, head : head + ROW, :].astype(F32)
+    both = (source, extra_source)
+    states = jnp.stack([lax.dynamic_slice(arrived, (at // PLANE * PLANE, 0, 0), (PLANE, head, LANES)) for at in both])
+    totals = jnp.concatenate([lax.dynamic_slice(arrived, (at, head, 0), (1, tail, LANES)) for at in both])
+    states = states.astype(F32)
+    totals = totals.astype(F32)
     return pl.pallas_call(
         final_kernel,
-        in_specs=[SMEM] + [VMEM] * 6,
+        in_specs=[SMEM] * 3 + [VMEM] * 7,
         out_specs=[VMEM] * 3,
         out_shape=[
             jax.ShapeDtypeStruct((homes + 1, width), BF16),
@@ -185,7 +242,7 @@
         scratch_shapes=[pltpu.VMEM((homes + 1, ROW, LANES), F32), pltpu.VMEM((3 * homes, width), F32)],
         compiler_params=pltpu.CompilerParams(vmem_limit_bytes=16 * 2**20),
         cost_estimate=cost(1 << 18),
-    )(scal, sums, extras, got, weights, first, second)
+    )(slot, adds, extra_adds, sums, extras, states, totals, weights, first, second)
 
 
 def solution(mesh):

time: 89.9 us -> 90.7 us (level)
  the two profiles are of different devices: /device:TPU:14 before, /device:TPU:10 now
where the time goes in v4:
time: 90.7 us; the launch traced here: 90.1 us
  starting transfers between devices  39.2 us (43%)
  waiting for transfers between devices  25.4 us (28%)
  between operations  8.73 us (10%)
  other arithmetic  5.36 us (6%)
  Pallas kernels  4.63 us (5%)
  blocking collectives  4.58 us (5%)
  local copies, waits for them, and re-layouts  2.16 us (2%)
    all_to_all x1, starting transfers between devices, per_device(): arrived = lax.all_to_all(outgoing.astype(F16), 'expert', 0, 0, tiled=True)  18.8 us
    ppermute x2, waiting for transfers between devices, share_states(): other = lax.ppermute(held, 'expert', [(i, i ^ bit) for i in range(devices)])  17 us
    all_to_all x1, starting transfers between devices, per_device(): parts = lax.all_to_all(partial, 'outer', 0, 0, tiled=True)  16.5 us
    all_to_all x1, waiting for transfers between devices, per_device(): arrived = lax.all_to_all(outgoing.astype(F16), 'expert', 0, 0, tiled=True)  8.46 us
    all_to_all x1, blocking collectives, per_device(): pair = lax.all_to_all(halves, 'core', 0, 0, tiled=True).astype(F32)  4.58 us
    ppermute x2, starting transfers between devices, share_states(): other = lax.ppermute(held, 'expert', [(i, i ^ bit) for i in range(devices)])  3.97 us
    pallas_call x1, Pallas kernels, per_device(): pl.pallas_call(final_kernel, in_specs=[SMEM] * 3 + [VMEM] * 7, out_specs=...  2.49 us
  transfers between devices with their start and end apart: 4, of which 3 were waited for; matrix products, arithmetic and copies ran while one was open for 4% of the time, Pallas kernels for 0%

profile of v4, /device:TPU:10, one launch (start us, length us, event | category | flops | bytes accessed | tf_op | source)
XLA Modules:
  0.0 90.1 jit_solution(3596297427331907340)
XLA Ops:
  0.6 0.0 copy-start
  0.6 1.5 %copy-done = bf16[1,9,57344]{2,1,0:T(8,128)(2,1)S(1)} copy-done((bf16[1,9,57344]{2,1,0:T(8,128)(2,1)S(1)}, bf16[1,9,57344]{2,1,0:T(8,128)(2,1)}, u32[]{:S(2)}) %copy-start) | copy-done | bytes 1032216
  2.1 0.6 shard_map.103
  2.7 4.6 %all_to_all.15 = bf16[2,16,128,128]{3,2,1,0:T(8,128)(2,1)S(1)} all-to-all(bf16[2,16,128,128]{3,2,1,0:T(8,128)(2,1)S(1)} %shard_map.103), channel_id=1, replica_groups=mesh['outer'=16,'core'=2,'expert'=32] {'core'}, dimensions={0} | all-to-all | bytes 2097152 | tf_op jit(solution)/shard_map/all_to_all | solution.py:206
  7.3 0.2 convert_element_type.42
  7.5 0.0 copy-start.3
  7.5 0.0 copy-start.1
  7.6 0.0 copy-start.2
  7.6 0.0 copy-start.4
  7.6 0.0 copy-start.5
  7.6 0.0 copy-start.6
  7.6 1.0 %fusion.2 = f16[16,128,128]{2,1,0:T(8,128)(2,1)} fusion(f32[2,16,128,128]{3,2,1,0:T(8,128)S(1)} %convert_element_type.42), kind=kLoop, calls=%fused_computation.4 | loop fusion | flops 786432 | bytes 2621440 | tf_op jit(solution)/shard_map/convert_element_type | solution.py:207
  8.6 16.5 %all-to-all-start.1 = ((f16[16,128,128]{2,1,0:T(8,128)(2,1)}), f16[16,128,128]{2,1,0:T(8,128)(2,1)S(1)}, u32[]{:S(2)}, u32[]{:S(2)}) async-start(f16[16,128,128]{2,1,0:T(8,128)(2,1)} %fusion.2), calls=%async_computation.1 | async-start | bytes 1048576 | tf_op jit(solution)/shard_map/all_to_all | solution.py:208
  25.0 0.0 copy-done.3
  25.0 0.0 copy-done.1
  25.0 0.0 copy-done.2
  25.1 1.9 %collective-permute-start = (f16[1,3,8,1792]{3,2,1,0:T(8,128)(2,1)S(1)}, f16[1,3,8,1792]{3,2,1,0:T(8,128)(2,1)S(1)}, u32[]{:S(2)}, u32[]{:S(2)}) collective-permute-start(f16[1,3,8,1792]{3,2,1,0:T(8,128)(2,1)S(1)} %fusion.3), channel_id=1, source_target_pairs={{0,2},{1,3},{2,0},{3,1},{4,6},{5,7},{6,4},{7,5},{8,10},{9,11},{10,... | collective-permute-start | bytes 258056 | tf_op jit(solution)/shard_map/ppermute | solution.py:191
  27.0 0.0 copy-done.4
  27.1 0.0 copy-done.5
  27.1 0.1 select_reduce_fusion.1
  27.2 0.0 copy-done.6
  27.2 0.2 select_reduce_fusion
  27.4 0.6 fusion.6
  28.0 0.7 fusion.7
  28.7 11.5 %collective-permute-done = f16[1,3,8,1792]{3,2,1,0:T(8,128)(2,1)S(1)} collective-permute-done((f16[1,3,8,1792]{3,2,1,0:T(8,128)(2,1)S(1)}, f16[1,3,8,1792]{3,2,1,0:T(8,128)(2,1)S(1)}, u32[]{:S(2)}, u32[]{:S(2)}) %collective-permute-start) | collective-permute-done | bytes 86048 | tf_op jit(solution)/shard_map/ppermute | solution.py:191
  40.3 2.0 %collective-permute-start.1 = (f16[2,3,8,1792]{3,2,1,0:T(8,128)(2,1)S(1)}, f16[2,3,8,1792]{3,2,1,0:T(8,128)(2,1)S(1)}, u32[]{:S(2)}, u32[]{:S(2)}) collective-permute-start(f16[2,3,8,1792]{3,2,1,0:T(8,128)(2,1)S(1)} %pad_maximum_fusion), channel_id=1, source_target_pairs={{0,1},{1,0},{2,3},{3,2},{4,5},{5,4},{6,7},{7,6},{8,9},{9,8},{10,11... | collective-permute-start | bytes 516104 | tf_op jit(solution)/shard_map/ppermute | solution.py:191
  42.3 0.6 and_select_fusion.1
  43.0 5.5 %collective-permute-done.1 = f16[2,3,8,1792]{3,2,1,0:T(8,128)(2,1)S(1)} collective-permute-done((f16[2,3,8,1792]{3,2,1,0:T(8,128)(2,1)S(1)}, f16[2,3,8,1792]{3,2,1,0:T(8,128)(2,1)S(1)}, u32[]{:S(2)}, u32[]{:S(2)}) %collective-permute-start.1) | collective-permute-done | bytes 172064 | tf_op jit(solution)/shard_map/ppermute | solution.py:191
  48.4 0.1 maximum_convert_fusion.held_ref
  48.5 0.0 all-to-all-done.1
  48.5 0.1 convert_reduce_fusion
  48.6 0.0 copy-start.7
  48.6 1.6 %shard_map.104 = f32[32,72,128]{2,1,0:T(8,128)S(1)} custom-call(s32[1]{0:T(128)} %bitcast.slot_ref, s32[1]{0:T(128)} %bitcast.3.mine_ref, s32[32]{0:T(128)S(1)} %get-tuple-element.16.asked_ref, s32[32]{0:T(128)S(1)} %get-tuple-element.17.moves_ref, s32[32]{0:T(128)S(1)} %get-tuple-element.15.wants_ref, f32[128,128]{1,0:T(8,128)S(1)} %broadcast_multiply_fusion.sums_ref, ...), custom_call_target="tpu_custom_call" | custom-call | flops 262144 | bytes 1048576 | tf_op jit(solution)/shard_map/pallas_call | solution.py:213
  50.2 0.9 convert_element_type.48
  51.1 18.8 %all-to-all-start.2 = ((f16[32,72,128]{2,1,0:T(8,128)(2,1)}), f16[32,72,128]{2,1,0:T(8,128)(2,1)S(1)}, u32[]{:S(2)}, u32[]{:S(2)}) async-start(f16[32,72,128]{2,1,0:T(8,128)(2,1)} %convert_element_type.48), calls=%async_computation.2 | async-start | bytes 1179648 | tf_op jit(solution)/shard_map/all_to_all | solution.py:226
  76.4 0.6 dynamic_slice.23
  78.3 0.0 copy-done.7
  78.3 0.1 select_reduce_fusion.3
  78.4 0.6 compare_convert_fusion.extra_adds_ref
  79.0 8.5 %all-to-all-done.2 = f16[32,72,128]{2,1,0:T(8,128)(2,1)S(1)} async-done(((f16[32,72,128]{2,1,0:T(8,128)(2,1)}), f16[32,72,128]{2,1,0:T(8,128)(2,1)S(1)}, u32[]{:S(2)}, u32[]{:S(2)}) %all-to-all-start.2) | async-done | bytes 589856 | tf_op jit(solution)/shard_map/all_to_all | solution.py:226
  87.6 2.5 %shard_map.105 = (bf16[9,1792]{1,0:T(8,128)(2,1)}, f32[8,1792]{1,0:T(8,128)}, f32[8,1792]{1,0:T(8,128)}) custom-call(s32[1]{0:T(128)} %bitcast.slot_ref, s32[32]{0:T(128)S(1)} %broadcast_add_fusion.adds_ref, s32[32]{0:T(128)S(1)} %compare_convert_fusion.extra_adds_ref, f32[128,128]{1,0:T(8,128)S(1)} %broadcast_multiply_fusion.sums_ref, ...), custom_call_target="tpu_custom_call" | custom-call | flops 262144 | bytes 1048576 | tf_op jit(solution)/shard_map/pallas_call | solution.py:233
  (12 shorter events, 0.2 us)
Async XLA Ops:
  0.6 1.5 %copy-start = (bf16[1,9,57344]{2,1,0:T(8,128)(2,1)S(1)}, bf16[1,9,57344]{2,1,0:T(8,128)(2,1)}, u32[]{:S(2)}) copy-start(bf16[1,9,57344]{2,1,0:T(8,128)(2,1)} %refs_0_.1) | copy-start | bytes 3096580
  7.5 17.5 %copy-start.3 = (bf16[8,1792]{1,0:T(8,128)(2,1)S(1)}, bf16[8,1792]{1,0:T(8,128)(2,1)}, u32[]{:S(2)}) copy-start(bf16[8,1792]{1,0:T(8,128)(2,1)} %w_ref.1) | copy-start | bytes 86020
  7.5 17.5 %copy-start.1 = (f32[8,1792]{1,0:T(8,128)S(1)}, f32[8,1792]{1,0:T(8,128)}, u32[]{:S(2)}) copy-start(f32[8,1792]{1,0:T(8,128)} %s_ref.1) | copy-start | bytes 172036
  7.6 17.5 %copy-start.2 = (f32[8,1792]{1,0:T(8,128)S(1)}, f32[8,1792]{1,0:T(8,128)}, u32[]{:S(2)}) copy-start(f32[8,1792]{1,0:T(8,128)} %f_ref.1) | copy-start | bytes 172036
  7.6 19.5 %copy-start.4 = (s32[256]{0:T(256)S(1)}, s32[256]{0:T(256)}, u32[]{:S(2)}) copy-start(s32[256]{0:T(256)} %param.12) | copy-start | bytes 3076
  7.6 19.5 %copy-start.5 = (s32[256]{0:T(256)S(1)}, s32[256]{0:T(256)}, u32[]{:S(2)}) copy-start(s32[256]{0:T(256)} %param.14) | copy-start | bytes 3076
  7.6 19.6 %copy-start.6 = (s32[32]{0:T(128)S(1)}, s32[32]{0:T(128)}, u32[]{:S(2)}) copy-start(s32[32]{0:T(128)} %param.15) | copy-start | bytes 388
  8.6 40.0 %all-to-all-start.1 = ((f16[16,128,128]{2,1,0:T(8,128)(2,1)}), f16[16,128,128]{2,1,0:T(8,128)(2,1)S(1)}, u32[]{:S(2)}, u32[]{:S(2)}) async-start(f16[16,128,128]{2,1,0:T(8,128)(2,1)} %fusion.2), calls=%async_computation.1 | async-start | bytes 1048576 | tf_op jit(solution)/shard_map/all_to_all | solution.py:208
  25.1 15.1 %collective-permute-start = (f16[1,3,8,1792]{3,2,1,0:T(8,128)(2,1)S(1)}, f16[1,3,8,1792]{3,2,1,0:T(8,128)(2,1)S(1)}, u32[]{:S(2)}, u32[]{:S(2)}) collective-permute-start(f16[1,3,8,1792]{3,2,1,0:T(8,128)(2,1)S(1)} %fusion.3), channel_id=1, source_target_pairs={{0,2},{1,3},{2,0},{3,1},{4,6},{5,7},{6,4},{7,5},{8,10},{9,11},{10,... | collective-permute-start | bytes 258056 | tf_op jit(solution)/shard_map/ppermute | solution.py:191
  40.3 8.2 %collective-permute-start.1 = (f16[2,3,8,1792]{3,2,1,0:T(8,128)(2,1)S(1)}, f16[2,3,8,1792]{3,2,1,0:T(8,128)(2,1)S(1)}, u32[]{:S(2)}, u32[]{:S(2)}) collective-permute-start(f16[2,3,8,1792]{3,2,1,0:T(8,128)(2,1)S(1)} %pad_maximum_fusion), channel_id=1, source_target_pairs={{0,1},{1,0},{2,3},{3,2},{4,5},{5,4},{6,7},{7,6},{8,9},{9,8},{10,11... | collective-permute-start | bytes 516104 | tf_op jit(solution)/shard_map/ppermute | solution.py:191
  48.6 29.7 %copy-start.7 = (s32[32]{0:T(128)S(1)}, s32[32]{0:T(128)}, u32[]{:S(2)}) copy-start(s32[32]{0:T(128)} %param.13) | copy-start | bytes 388
  51.1 36.4 %all-to-all-start.2 = ((f16[32,72,128]{2,1,0:T(8,128)(2,1)}), f16[32,72,128]{2,1,0:T(8,128)(2,1)S(1)}, u32[]{:S(2)}, u32[]{:S(2)}) async-start(f16[32,72,128]{2,1,0:T(8,128)(2,1)} %convert_element_type.48), calls=%async_computation.2 | async-start | bytes 1179648 | tf_op jit(solution)/shard_map/all_to_all | solution.py:226

commit v5 on v4

--- a/solution.py
+++ b/solution.py
@@ -161,6 +161,10 @@
         nw_ref[:, cols] = jnp.concatenate([updated, extra], axis=0).astype(BF16)
 
 
+def plane_stride():
+    return max(lax.axis_size("expert") // 8, 1)
+
+
 def routes(homes, old_home, old_extra, new_home, new_extra):
     me = lax.axis_index("expert")
     my_new = lax.dynamic_slice_in_dim(new_home, me * homes, homes)
@@ -179,15 +183,20 @@
     asked = jnp.where(wants // homes == me, wants % homes, 0)
     adds = jnp.sum(jnp.where(old_extra[:, None] == my_new[None, :], ids[None, :] + 1, 0), axis=1) - 1
     extra_adds = (old_extra == wanted).astype(jnp.int32)
-    plane = PLANE * homes
-    return slot, source, extra_source, asked, moves % plane, wants % plane, adds, extra_adds
+    stride = plane_stride()
+
+    def in_plane(place):
+        return (place // homes // stride) % PLANE * homes + place % homes
+
+    return slot, source, extra_source, asked, in_plane(moves), in_plane(wants), adds, extra_adds
 
 
 def share_states(weights, first, second):
     devices = lax.axis_size("expert")
     states = jnp.stack([weights.astype(F32), first, second])
     held = (states * STATE_SCALE).astype(F16)[None]
-    for bit in (2, 1):
+    for step in (2, 1):
+        bit = step * plane_stride()
         other = lax.ppermute(held, "expert", [(i, i ^ bit) for i in range(devices)])
         held = jnp.concatenate([held, other], axis=0)
     return held.astype(F32)
@@ -201,7 +210,7 @@
     tables = routes(homes, old_home, old_extra, new_home, new_extra)
     slot, source, extra_source, asked, moves, wants, adds, extra_adds = tables
     held = share_states(weights, first, second)
-    mine = (lax.axis_index("expert") % PLANE).astype(jnp.int32).reshape(1)
+    mine = (lax.axis_index("expert") // plane_stride() % PLANE).astype(jnp.int32).reshape(1)
     halves = split_by_core(grads, outer, width)
     pair = lax.all_to_all(halves, "core", 0, 0, tiled=True).astype(F32)
     partial = ((pair[0] + pair[1]) * PAIR_SCALE).astype(F16)
@@ -226,7 +235,11 @@
     arrived = lax.all_to_all(outgoing.astype(F16), "expert", 0, 0, tiled=True)
     extras = arrived[:, head : head + ROW, :].astype(F32)
     both = (source, extra_source)
-    states = jnp.stack([lax.dynamic_slice(arrived, (at // PLANE * PLANE, 0, 0), (PLANE, head, LANES)) for at in both])
+    stride = plane_stride()
+    planes = arrived.reshape(devices // (PLANE * stride), PLANE, stride, head + tail, LANES)
+    size = (1, PLANE, 1, head, LANES)
+    states = [lax.dynamic_slice(planes, (at // (PLANE * stride), 0, at % stride, 0, 0), size) for at in both]
+    states = jnp.stack(states).reshape(2, PLANE, head, LANES)
     totals = jnp.concatenate([lax.dynamic_slice(arrived, (at, head, 0), (1, tail, LANES)) for at in both])
     states = states.astype(F32)
     totals = totals.astype(F32)

time: 90.7 us -> 81.2 us (0.90)
  the two profiles are of different devices: /device:TPU:10 before, /device:TPU:14 now
where the time goes in v5:
time: 81.2 us; the launch traced here: 80.6 us
  starting transfers between devices  39.4 us (49%)
  waiting for transfers between devices  15.7 us (19%)
  between operations  8.77 us (11%)
  other arithmetic  5.38 us (7%)
  Pallas kernels  4.62 us (6%)
  blocking collectives  4.58 us (6%)
  local copies, waits for them, and re-layouts  2.16 us (3%)
    all_to_all x1, starting transfers between devices, per_device(): parts = lax.all_to_all(partial, 'outer', 0, 0, tiled=True)  16.4 us
    all_to_all x1, starting transfers between devices, per_device(): arrived = lax.all_to_all(outgoing.astype(F16), 'expert', 0, 0, tiled=True)  13.9 us
    ppermute x2, starting transfers between devices, share_states(): other = lax.ppermute(held, 'expert', [(i, i ^ bit) for i in range(devices)])  9.07 us
    all_to_all x1, waiting for transfers between devices, per_device(): arrived = lax.all_to_all(outgoing.astype(F16), 'expert', 0, 0, tiled=True)  8.09 us
    all_to_all x1, blocking collectives, per_device(): pair = lax.all_to_all(halves, 'core', 0, 0, tiled=True).astype(F32)  4.58 us
    ppermute x2, waiting for transfers between devices, share_states(): other = lax.ppermute(held, 'expert', [(i, i ^ bit) for i in range(devices)])  4.27 us
    all_to_all x1, waiting for transfers between devices, per_device(): parts = lax.all_to_all(partial, 'outer', 0, 0, tiled=True)  3.35 us
    pallas_call x1, Pallas kernels, per_device(): pl.pallas_call(final_kernel, in_specs=[SMEM] * 3 + [VMEM] * 7, out_specs=...  2.49 us
  transfers between devices with their start and end apart: 4, of which 4 were waited for; matrix products, arithmetic and copies ran while one was open for 5% of the time, Pallas kernels for 0%

profile of v5, /device:TPU:14, one launch (start us, length us, event | category | flops | bytes accessed | tf_op | source)
XLA Modules:
  0.0 80.6 jit_solution(15154780084120681003)
XLA Ops:
  0.6 0.0 copy-start
  0.6 1.5 %copy-done = bf16[1,9,57344]{2,1,0:T(8,128)(2,1)S(1)} copy-done((bf16[1,9,57344]{2,1,0:T(8,128)(2,1)S(1)}, bf16[1,9,57344]{2,1,0:T(8,128)(2,1)}, u32[]{:S(2)}) %copy-start) | copy-done | bytes 1032216
  2.1 0.6 shard_map.103
  2.7 4.6 %all_to_all.15 = bf16[2,16,128,128]{3,2,1,0:T(8,128)(2,1)S(1)} all-to-all(bf16[2,16,128,128]{3,2,1,0:T(8,128)(2,1)S(1)} %shard_map.103), channel_id=1, replica_groups=mesh['outer'=16,'core'=2,'expert'=32] {'core'}, dimensions={0} | all-to-all | bytes 2097152 | tf_op jit(solution)/shard_map/all_to_all | solution.py:215
  7.3 0.2 convert_element_type.44
  7.5 0.0 copy-start.3
  7.5 0.0 copy-start.1
  7.6 0.0 copy-start.2
  7.6 0.0 copy-start.4
  7.6 0.0 copy-start.5
  7.6 0.0 copy-start.6
  7.6 1.0 %fusion.2 = f16[16,128,128]{2,1,0:T(8,128)(2,1)} fusion(f32[2,16,128,128]{3,2,1,0:T(8,128)S(1)} %convert_element_type.44), kind=kLoop, calls=%fused_computation.4 | loop fusion | flops 786432 | bytes 2621440 | tf_op jit(solution)/shard_map/convert_element_type | solution.py:216
  8.6 16.4 %all-to-all-start.1 = ((f16[16,128,128]{2,1,0:T(8,128)(2,1)}), f16[16,128,128]{2,1,0:T(8,128)(2,1)S(1)}, u32[]{:S(2)}, u32[]{:S(2)}) async-start(f16[16,128,128]{2,1,0:T(8,128)(2,1)} %fusion.2), calls=%async_computation.1 | async-start | bytes 1048576 | tf_op jit(solution)/shard_map/all_to_all | solution.py:217
  25.0 0.0 copy-done.3
  25.0 0.0 copy-done.1
  25.0 0.0 copy-done.2
  25.0 4.3 %collective-permute-start = (f16[1,3,8,1792]{3,2,1,0:T(8,128)(2,1)S(1)}, f16[1,3,8,1792]{3,2,1,0:T(8,128)(2,1)S(1)}, u32[]{:S(2)}, u32[]{:S(2)}) collective-permute-start(f16[1,3,8,1792]{3,2,1,0:T(8,128)(2,1)S(1)} %fusion.3), channel_id=1, source_target_pairs={{0,8},{1,9},{2,10},{3,11},{4,12},{5,13},{6,14},{7,15},{8,0},{9,1},... | collective-permute-start | bytes 258056 | tf_op jit(solution)/shard_map/ppermute | solution.py:200
  29.4 0.0 copy-done.4
  29.4 0.0 copy-done.5
  29.5 0.1 select_reduce_fusion.1
  29.6 0.0 copy-done.6
  29.6 0.2 select_reduce_fusion
  29.8 0.6 fusion.8
  30.4 0.6 fusion.7
  31.1 0.7 fusion.9
  31.8 0.6 collective-permute-done
  32.4 4.7 %collective-permute-start.1 = (f16[2,3,8,1792]{3,2,1,0:T(8,128)(2,1)S(1)}, f16[2,3,8,1792]{3,2,1,0:T(8,128)(2,1)S(1)}, u32[]{:S(2)}, u32[]{:S(2)}) collective-permute-start(f16[2,3,8,1792]{3,2,1,0:T(8,128)(2,1)S(1)} %pad_maximum_fusion), channel_id=1, source_target_pairs={{0,4},{1,5},{2,6},{3,7},{4,0},{5,1},{6,2},{7,3},{8,12},{9,13},{10,... | collective-permute-start | bytes 516104 | tf_op jit(solution)/shard_map/ppermute | solution.py:200
  37.1 3.7 %collective-permute-done.1 = f16[2,3,8,1792]{3,2,1,0:T(8,128)(2,1)S(1)} collective-permute-done((f16[2,3,8,1792]{3,2,1,0:T(8,128)(2,1)S(1)}, f16[2,3,8,1792]{3,2,1,0:T(8,128)(2,1)S(1)}, u32[]{:S(2)}, u32[]{:S(2)}) %collective-permute-start.1) | collective-permute-done | bytes 172064 | tf_op jit(solution)/shard_map/ppermute | solution.py:200
  40.8 0.1 maximum_convert_fusion.held_ref
  40.9 3.4 %all-to-all-done.1 = f16[16,128,128]{2,1,0:T(8,128)(2,1)S(1)} async-done(((f16[16,128,128]{2,1,0:T(8,128)(2,1)}), f16[16,128,128]{2,1,0:T(8,128)(2,1)S(1)}, u32[]{:S(2)}, u32[]{:S(2)}) %all-to-all-start.1) | async-done | bytes 524320 | tf_op jit(solution)/shard_map/all_to_all | solution.py:217
  44.2 0.1 convert_reduce_fusion
  44.3 0.0 copy-start.7
  44.4 1.6 %shard_map.104 = f32[32,72,128]{2,1,0:T(8,128)S(1)} custom-call(s32[1]{0:T(128)} %bitcast.slot_ref, s32[1]{0:T(128)} %bitcast.3.mine_ref, s32[32]{0:T(128)S(1)} %get-tuple-element.17.asked_ref, s32[32]{0:T(128)S(1)} %get-tuple-element.18.moves_ref, s32[32]{0:T(128)S(1)} %get-tuple-element.16.wants_ref, f32[128,128]{1,0:T(8,128)S(1)} %broadcast_multiply_fusion.sums_ref, ...), custom_call_target="tpu_custom_call" | custom-call | flops 262144 | bytes 1048576 | tf_op jit(solution)/shard_map/pallas_call | solution.py:222
  45.9 0.9 %convert_element_type.50 = f16[32,72,128]{2,1,0:T(8,128)(2,1)} convert(f32[32,72,128]{2,1,0:T(8,128)S(1)} %shard_map.104) | non-fusion elementwise | flops 294912 | bytes 1769472 | tf_op jit(solution)/shard_map/convert_element_type | solution.py:235
  46.8 13.9 %all-to-all-start.2 = ((f16[32,72,128]{2,1,0:T(8,128)(2,1)}), f16[32,72,128]{2,1,0:T(8,128)(2,1)S(1)}, u32[]{:S(2)}, u32[]{:S(2)}) async-start(f16[32,72,128]{2,1,0:T(8,128)(2,1)} %convert_element_type.50), calls=%async_computation.2 | async-start | bytes 1179648 | tf_op jit(solution)/shard_map/all_to_all | solution.py:235
  67.3 0.6 dynamic_slice.23
  69.2 0.0 copy-done.7
  69.2 0.1 select_reduce_fusion.3
  69.3 0.6 compare_convert_fusion.extra_adds_ref
  69.9 8.1 %all-to-all-done.2 = f16[32,72,128]{2,1,0:T(8,128)(2,1)S(1)} async-done(((f16[32,72,128]{2,1,0:T(8,128)(2,1)}), f16[32,72,128]{2,1,0:T(8,128)(2,1)S(1)}, u32[]{:S(2)}, u32[]{:S(2)}) %all-to-all-start.2) | async-done | bytes 589856 | tf_op jit(solution)/shard_map/all_to_all | solution.py:235
  78.1 2.5 %shard_map.105 = (bf16[9,1792]{1,0:T(8,128)(2,1)}, f32[8,1792]{1,0:T(8,128)}, f32[8,1792]{1,0:T(8,128)}) custom-call(s32[1]{0:T(128)} %bitcast.slot_ref, s32[32]{0:T(128)S(1)} %broadcast_add_fusion.adds_ref, s32[32]{0:T(128)S(1)} %compare_convert_fusion.extra_adds_ref, f32[128,128]{1,0:T(8,128)S(1)} %broadcast_multiply_fusion.sums_ref, ...), custom_call_target="tpu_custom_call" | custom-call | flops 262144 | bytes 1048576 | tf_op jit(solution)/shard_map/pallas_call | solution.py:246
  (13 shorter events, 0.2 us)
Async XLA Ops:
  0.6 1.5 %copy-start = (bf16[1,9,57344]{2,1,0:T(8,128)(2,1)S(1)}, bf16[1,9,57344]{2,1,0:T(8,128)(2,1)}, u32[]{:S(2)}) copy-start(bf16[1,9,57344]{2,1,0:T(8,128)(2,1)} %refs_0_.1) | copy-start | bytes 3096580
  7.5 17.4 %copy-start.3 = (bf16[8,1792]{1,0:T(8,128)(2,1)S(1)}, bf16[8,1792]{1,0:T(8,128)(2,1)}, u32[]{:S(2)}) copy-start(bf16[8,1792]{1,0:T(8,128)(2,1)} %w_ref.1) | copy-start | bytes 86020
  7.5 17.5 %copy-start.1 = (f32[8,1792]{1,0:T(8,128)S(1)}, f32[8,1792]{1,0:T(8,128)}, u32[]{:S(2)}) copy-start(f32[8,1792]{1,0:T(8,128)} %s_ref.1) | copy-start | bytes 172036
  7.6 17.4 %copy-start.2 = (f32[8,1792]{1,0:T(8,128)S(1)}, f32[8,1792]{1,0:T(8,128)}, u32[]{:S(2)}) copy-start(f32[8,1792]{1,0:T(8,128)} %f_ref.1) | copy-start | bytes 172036
  7.6 21.9 %copy-start.4 = (s32[256]{0:T(256)S(1)}, s32[256]{0:T(256)}, u32[]{:S(2)}) copy-start(s32[256]{0:T(256)} %param.12) | copy-start | bytes 3076
  7.6 21.9 %copy-start.5 = (s32[256]{0:T(256)S(1)}, s32[256]{0:T(256)}, u32[]{:S(2)}) copy-start(s32[256]{0:T(256)} %param.14) | copy-start | bytes 3076
  7.6 22.0 %copy-start.6 = (s32[32]{0:T(128)S(1)}, s32[32]{0:T(128)}, u32[]{:S(2)}) copy-start(s32[32]{0:T(128)} %param.15) | copy-start | bytes 388
  8.6 35.7 %all-to-all-start.1 = ((f16[16,128,128]{2,1,0:T(8,128)(2,1)}), f16[16,128,128]{2,1,0:T(8,128)(2,1)S(1)}, u32[]{:S(2)}, u32[]{:S(2)}) async-start(f16[16,128,128]{2,1,0:T(8,128)(2,1)} %fusion.2), calls=%async_computation.1 | async-start | bytes 1048576 | tf_op jit(solution)/shard_map/all_to_all | solution.py:217
  25.0 7.3 %collective-permute-start = (f16[1,3,8,1792]{3,2,1,0:T(8,128)(2,1)S(1)}, f16[1,3,8,1792]{3,2,1,0:T(8,128)(2,1)S(1)}, u32[]{:S(2)}, u32[]{:S(2)}) collective-permute-start(f16[1,3,8,1792]{3,2,1,0:T(8,128)(2,1)S(1)} %fusion.3), channel_id=1, source_target_pairs={{0,8},{1,9},{2,10},{3,11},{4,12},{5,13},{6,14},{7,15},{8,0},{9,1},... | collective-permute-start | bytes 258056 | tf_op jit(solution)/shard_map/ppermute | solution.py:200
  32.4 8.5 %collective-permute-start.1 = (f16[2,3,8,1792]{3,2,1,0:T(8,128)(2,1)S(1)}, f16[2,3,8,1792]{3,2,1,0:T(8,128)(2,1)S(1)}, u32[]{:S(2)}, u32[]{:S(2)}) collective-permute-start(f16[2,3,8,1792]{3,2,1,0:T(8,128)(2,1)S(1)} %pad_maximum_fusion), channel_id=1, source_target_pairs={{0,4},{1,5},{2,6},{3,7},{4,0},{5,1},{6,2},{7,3},{8,12},{9,13},{10,... | collective-permute-start | bytes 516104 | tf_op jit(solution)/shard_map/ppermute | solution.py:200
  44.3 24.8 %copy-start.7 = (s32[32]{0:T(128)S(1)}, s32[32]{0:T(128)}, u32[]{:S(2)}) copy-start(s32[32]{0:T(128)} %param.13) | copy-start | bytes 388
  46.8 31.2 %all-to-all-start.2 = ((f16[32,72,128]{2,1,0:T(8,128)(2,1)}), f16[32,72,128]{2,1,0:T(8,128)(2,1)S(1)}, u32[]{:S(2)}, u32[]{:S(2)}) async-start(f16[32,72,128]{2,1,0:T(8,128)(2,1)} %convert_element_type.50), calls=%async_computation.2 | async-start | bytes 1179648 | tf_op jit(solution)/shard_map/all_to_all | solution.py:235

commit v6 on v5

--- a/solution.py
+++ b/solution.py
@@ -64,9 +64,9 @@
     return per, [min(y * per, tiles - per) for y in range(PLANE)]
 
 
-def rows_kernel(slot_ref, mine_ref, asked_ref, moves_ref, wants_ref, sums_ref, held_ref, out_ref, state_a, state_b, sent):
-    homes = sent.shape[0]
-    tiles = held_ref.shape[3] // LANES
+def states_kernel(mine_ref, moves_ref, wants_ref, held_ref, out_ref, state_a, state_b):
+    homes, width = held_ref.shape[2:]
+    tiles = width // LANES
     per, _ = starts(tiles)
     mine = mine_ref[0]
     first_tile = jnp.minimum(mine * per, tiles - per)
@@ -81,24 +81,31 @@
                 for i in range(homes):
                     state_a[base + i, n * per + k : n * per + k + 1, :] = value[i : i + 1, :]
                     state_b[base + i, (3 + n) * per + k : (3 + n) * per + k + 1, :] = value[i : i + 1, :]
-    sums = sums_ref[...] * SUM_SCALE
+    for d in range(out_ref.shape[0]):
+        out_ref[d] = state_a[moves_ref[d]] + state_b[wants_ref[d]]
+
+
+def sums_kernel(slot_ref, asked_ref, sums_ref, heads_ref, out_ref, home, fixed):
+    homes = home.shape[0]
+    tiles = (sums_ref.shape[0] - ROW) // homes
+    home[...] = jnp.zeros_like(home)
+    fixed[...] = jnp.zeros_like(fixed)
     slot = slot_ref[0]
-    sent[...] = jnp.zeros_like(sent)
-    for i in range(homes):
-        for t in range(tiles):
-            sent[i, tiles + t : tiles + t + 1, :] = sums[t * homes + i : t * homes + i + 1, :]
-    leaving = sent[slot]
-    for t in range(tiles):
+    for t in range(tiles):
+        tile = sums_ref[t * homes : (t + 1) * homes, :] * SUM_SCALE
+        row = 2 * tiles + t
+        for i in range(homes):
+            home[i, row : row + 1, :] = tile[i : i + 1, :]
         at = tiles * homes + t
-        for i in range(homes):
-            row = 2 * tiles + t
-            sent[i, row : row + 1, :] = sent[i, tiles + t : tiles + t + 1, :]
-            sent[i, tiles + t : tiles + t + 1, :] = leaving[tiles + t : tiles + t + 1, :]
-            sent[i, t : t + 1, :] = sums[at : at + 1, :]
-    head = 6 * per
+        fixed[t : t + 1, :] = sums_ref[at : at + 1, :] * SUM_SCALE
+    for t in range(tiles):
+        row = 2 * tiles + t
+        fixed[tiles + t : tiles + t + 1, :] = home[slot, row : row + 1, :]
+    keep = fixed[...]
+    head = heads_ref.shape[1]
     for d in range(out_ref.shape[0]):
-        out_ref[d, :head, :] = state_a[moves_ref[d]] + state_b[wants_ref[d]]
-        out_ref[d, head:, :] = sent[asked_ref[d]]
+        out_ref[d, :head, :] = heads_ref[d]
+        out_ref[d, head:, :] = keep + home[asked_ref[d]]
 
 
 def adam(total, base, first, second):
@@ -116,17 +123,11 @@
     per, firsts = starts(tiles)
     slot = slot_ref[0]
     acc[...] = jnp.zeros_like(acc)
+    copied = jnp.zeros(acc.shape[1:], F32)
     for s in range(extras_ref.shape[0]):
-        to = adds_ref[s]
-
-        @pl.when(to >= 0)
-        def _():
-            acc[to] += extras_ref[s]
-
-        @pl.when(extra_adds_ref[s] > 0)
-        def _():
-            acc[homes] += extras_ref[s]
-
+        acc[adds_ref[s]] += extras_ref[s]
+        copied += extras_ref[s] * extra_adds_ref[s].astype(F32)
+    acc[homes] = copied
     for y in range(PLANE):
         for k in range(per):
             cols = slice((firsts[y] + k) * LANES, (firsts[y] + k + 1) * LANES)
@@ -181,7 +182,8 @@
     source = jnp.sum(jnp.where(device == me, moves // homes, 0))
     extra_source = jnp.sum(jnp.where(device == me, wants // homes, 0))
     asked = jnp.where(wants // homes == me, wants % homes, 0)
-    adds = jnp.sum(jnp.where(old_extra[:, None] == my_new[None, :], ids[None, :] + 1, 0), axis=1) - 1
+    spare = homes + 1
+    adds = jnp.sum(jnp.where(old_extra[:, None] == my_new[None, :], ids[None, :] - spare, 0), axis=1) + spare
     extra_adds = (old_extra == wanted).astype(jnp.int32)
     stride = plane_stride()
 
@@ -211,27 +213,32 @@
     slot, source, extra_source, asked, moves, wants, adds, extra_adds = tables
     held = share_states(weights, first, second)
     mine = (lax.axis_index("expert") // plane_stride() % PLANE).astype(jnp.int32).reshape(1)
+    per, _ = starts(tiles)
+    head = 6 * per
+    tail = -(-3 * tiles // 8) * 8
+    heads = pl.pallas_call(
+        states_kernel,
+        in_specs=[SMEM] * 3 + [VMEM],
+        out_specs=VMEM,
+        out_shape=jax.ShapeDtypeStruct((devices, head, LANES), F32),
+        scratch_shapes=[pltpu.VMEM((PLANE * homes, head, LANES), F32)] * 2,
+        compiler_params=pltpu.CompilerParams(vmem_limit_bytes=16 * 2**20),
+        cost_estimate=cost(1 << 18),
+    )(mine, moves, wants, held)
     halves = split_by_core(grads, outer, width)
     pair = lax.all_to_all(halves, "core", 0, 0, tiled=True).astype(F32)
     partial = ((pair[0] + pair[1]) * PAIR_SCALE).astype(F16)
     parts = lax.all_to_all(partial, "outer", 0, 0, tiled=True)
     sums = jnp.sum(parts.astype(F32), axis=0) * (1.0 / PAIR_SCALE)
-    per, _ = starts(tiles)
-    head = 6 * per
-    tail = -(-3 * tiles // 8) * 8
     outgoing = pl.pallas_call(
-        rows_kernel,
-        in_specs=[SMEM] * 5 + [VMEM] * 2,
+        sums_kernel,
+        in_specs=[SMEM] * 2 + [VMEM] * 2,
         out_specs=VMEM,
         out_shape=jax.ShapeDtypeStruct((devices, head + tail, LANES), F32),
-        scratch_shapes=[
-            pltpu.VMEM((PLANE * homes, head, LANES), F32),
-            pltpu.VMEM((PLANE * homes, head, LANES), F32),
-            pltpu.VMEM((homes, tail, LANES), F32),
-        ],
+        scratch_shapes=[pltpu.VMEM((homes, tail, LANES), F32), pltpu.VMEM((tail, LANES), F32)],
         compiler_params=pltpu.CompilerParams(vmem_limit_bytes=16 * 2**20),
         cost_estimate=cost(1 << 18),
-    )(slot, mine, asked, moves, wants, sums, held)
+    )(slot, asked, sums, heads)
     arrived = lax.all_to_all(outgoing.astype(F16), "expert", 0, 0, tiled=True)
     extras = arrived[:, head : head + ROW, :].astype(F32)
     both = (source, extra_source)
@@ -252,7 +259,7 @@
             jax.ShapeDtypeStruct((homes, width), F32),
             jax.ShapeDtypeStruct((homes, width), F32),
         ],
-        scratch_shapes=[pltpu.VMEM((homes + 1, ROW, LANES), F32), pltpu.VMEM((3 * homes, width), F32)],
+        scratch_shapes=[pltpu.VMEM((homes + 2, ROW, LANES), F32), pltpu.VMEM((3 * homes, width), F32)],
         compiler_params=pltpu.CompilerParams(vmem_limit_bytes=16 * 2**20),
         cost_estimate=cost(1 << 18),
     )(slot, adds, extra_adds, sums, extras, states, totals, weights, first, second)

time: 81.2 us -> 80.5 us (level)
    all_to_all x1, waiting for transfers between devices: 3.35 us -> 2.51 us  [per_device(): parts = lax.all_to_all(partial, 'outer', 0, 0, tiled=True)]
    pallas_call x1 -> x2, Pallas kernels: 1.55 us -> 2.07 us  [the longest x1 1.22 us: per_device(): pl.pallas_call(sums_kernel, in_specs=[SMEM] * 2 + [VMEM] * 2, out_specs=V...]
  transfers between devices with their start and end apart: 4 -> 4, of which waited for: 4 -> 4; matrix products, arithmetic and copies ran while one was open for 5% -> 5% of each run, Pallas kernels for 0% -> 1%
where the time goes in v6:
time: 80.5 us; the launch traced here: 79.9 us
  starting transfers between devices  39.4 us (49%)
  waiting for transfers between devices  14.9 us (19%)
  between operations  8.77 us (11%)
  other arithmetic  5.37 us (7%)
  Pallas kernels  4.79 us (6%)
  blocking collectives  4.58 us (6%)
  local copies, waits for them, and re-layouts  2.16 us (3%)
    all_to_all x1, starting transfers between devices, per_device(): parts = lax.all_to_all(partial, 'outer', 0, 0, tiled=True)  16.4 us
    all_to_all x1, starting transfers between devices, per_device(): arrived = lax.all_to_all(outgoing.astype(F16), 'expert', 0, 0, tiled=True)  13.9 us
    ppermute x2, starting transfers between devices, share_states(): other = lax.ppermute(held, 'expert', [(i, i ^ bit) for i in range(devices)])  9.07 us
    all_to_all x1, waiting for transfers between devices, per_device(): arrived = lax.all_to_all(outgoing.astype(F16), 'expert', 0, 0, tiled=True)  8.09 us
    all_to_all x1, blocking collectives, per_device(): pair = lax.all_to_all(halves, 'core', 0, 0, tiled=True).astype(F32)  4.58 us
    ppermute x2, waiting for transfers between devices, share_states(): other = lax.ppermute(held, 'expert', [(i, i ^ bit) for i in range(devices)])  4.27 us
    all_to_all x1, waiting for transfers between devices, per_device(): parts = lax.all_to_all(partial, 'outer', 0, 0, tiled=True)  2.51 us
    pallas_call x1, Pallas kernels, per_device(): pl.pallas_call(final_kernel, in_specs=[SMEM] * 3 + [VMEM] * 7, out_specs=...  2.14 us
  transfers between devices with their start and end apart: 4, of which 4 were waited for; matrix products, arithmetic and copies ran while one was open for 5% of the time, Pallas kernels for 1%

profile of v6, /device:TPU:14, one launch (start us, length us, event | category | flops | bytes accessed | tf_op | source)
XLA Modules:
  0.0 79.9 jit_solution(12550885045504256623)
XLA Ops:
  0.6 0.0 copy-start
  0.6 1.5 %copy-done = bf16[1,9,57344]{2,1,0:T(8,128)(2,1)S(1)} copy-done((bf16[1,9,57344]{2,1,0:T(8,128)(2,1)S(1)}, bf16[1,9,57344]{2,1,0:T(8,128)(2,1)}, u32[]{:S(2)}) %copy-start) | copy-done | bytes 1032216
  2.1 0.6 shard_map.103
  2.7 4.6 %all_to_all.15 = bf16[2,16,128,128]{3,2,1,0:T(8,128)(2,1)S(1)} all-to-all(bf16[2,16,128,128]{3,2,1,0:T(8,128)(2,1)S(1)} %shard_map.103), channel_id=1, replica_groups=mesh['outer'=16,'core'=2,'expert'=32] {'core'}, dimensions={0} | all-to-all | bytes 2097152 | tf_op jit(solution)/shard_map/all_to_all | solution.py:229
  7.3 0.2 convert_element_type.44
  7.5 0.0 copy-start.3
  7.5 0.0 copy-start.1
  7.6 0.0 copy-start.2
  7.6 0.0 copy-start.4
  7.6 0.0 copy-start.5
  7.6 0.0 copy-start.6
  7.6 1.0 %fusion.2 = f16[16,128,128]{2,1,0:T(8,128)(2,1)} fusion(f32[2,16,128,128]{3,2,1,0:T(8,128)S(1)} %convert_element_type.44), kind=kLoop, calls=%fused_computation.4 | loop fusion | flops 786432 | bytes 2621440 | tf_op jit(solution)/shard_map/convert_element_type | solution.py:230
  8.6 16.4 %all-to-all-start.1 = ((f16[16,128,128]{2,1,0:T(8,128)(2,1)}), f16[16,128,128]{2,1,0:T(8,128)(2,1)S(1)}, u32[]{:S(2)}, u32[]{:S(2)}) async-start(f16[16,128,128]{2,1,0:T(8,128)(2,1)} %fusion.2), calls=%async_computation.1 | async-start | bytes 1048576 | tf_op jit(solution)/shard_map/all_to_all | solution.py:231
  25.0 0.0 copy-done.3
  25.0 0.0 copy-done.1
  25.0 0.0 copy-done.2
  25.0 4.3 %collective-permute-start = (f16[1,3,8,1792]{3,2,1,0:T(8,128)(2,1)S(1)}, f16[1,3,8,1792]{3,2,1,0:T(8,128)(2,1)S(1)}, u32[]{:S(2)}, u32[]{:S(2)}) collective-permute-start(f16[1,3,8,1792]{3,2,1,0:T(8,128)(2,1)S(1)} %fusion.3), channel_id=1, source_target_pairs={{0,8},{1,9},{2,10},{3,11},{4,12},{5,13},{6,14},{7,15},{8,0},{9,1},... | collective-permute-start | bytes 258056 | tf_op jit(solution)/shard_map/ppermute | solution.py:202
  29.4 0.0 copy-done.4
  29.4 0.0 copy-done.5
  29.5 0.1 select_reduce_fusion.1
  29.6 0.0 copy-done.6
  29.6 0.2 select_reduce_fusion
  29.8 0.6 fusion.8
  30.4 0.6 fusion.7
  31.1 0.7 fusion.9
  31.8 0.6 collective-permute-done
  32.4 4.7 %collective-permute-start.1 = (f16[2,3,8,1792]{3,2,1,0:T(8,128)(2,1)S(1)}, f16[2,3,8,1792]{3,2,1,0:T(8,128)(2,1)S(1)}, u32[]{:S(2)}, u32[]{:S(2)}) collective-permute-start(f16[2,3,8,1792]{3,2,1,0:T(8,128)(2,1)S(1)} %pad_maximum_fusion), channel_id=1, source_target_pairs={{0,4},{1,5},{2,6},{3,7},{4,0},{5,1},{6,2},{7,3},{8,12},{9,13},{10,... | collective-permute-start | bytes 516104 | tf_op jit(solution)/shard_map/ppermute | solution.py:202
  37.1 3.7 %collective-permute-done.1 = f16[2,3,8,1792]{3,2,1,0:T(8,128)(2,1)S(1)} collective-permute-done((f16[2,3,8,1792]{3,2,1,0:T(8,128)(2,1)S(1)}, f16[2,3,8,1792]{3,2,1,0:T(8,128)(2,1)S(1)}, u32[]{:S(2)}, u32[]{:S(2)}) %collective-permute-start.1) | collective-permute-done | bytes 172064 | tf_op jit(solution)/shard_map/ppermute | solution.py:202
  40.8 0.1 maximum_convert_fusion.held_ref
  40.9 0.8 %shard_map.104.heads_ref = f32[32,24,128]{2,1,0:T(8,128)S(1)} custom-call(s32[1]{0:T(128)} %bitcast.3.mine_ref, s32[32]{0:T(128)S(1)} %get-tuple-element.18.moves_ref, s32[32]{0:T(128)S(1)} %get-tuple-element.16.wants_ref, f32[4,3,8,1792]{3,2,1,0:T(8,128)S(1)} %maximum_convert_fusion.held_ref), custom_call_target="tpu_custom_call" | custom-call | flops 262144 | bytes 1048576 | tf_op jit(solution)/shard_map/pallas_call | solution.py:219
  41.7 2.5 %all-to-all-done.1 = f16[16,128,128]{2,1,0:T(8,128)(2,1)S(1)} async-done(((f16[16,128,128]{2,1,0:T(8,128)(2,1)}), f16[16,128,128]{2,1,0:T(8,128)(2,1)S(1)}, u32[]{:S(2)}, u32[]{:S(2)}) %all-to-all-start.1) | async-done | bytes 524320 | tf_op jit(solution)/shard_map/all_to_all | solution.py:231
  44.2 0.1 convert_reduce_fusion
  44.3 0.0 copy-start.7
  44.4 1.2 %shard_map.105 = f32[32,72,128]{2,1,0:T(8,128)S(1)} custom-call(s32[1]{0:T(128)} %bitcast.slot_ref, s32[32]{0:T(128)S(1)} %get-tuple-element.17.asked_ref, f32[128,128]{1,0:T(8,128)S(1)} %broadcast_multiply_fusion.sums_ref, f32[32,24,128]{2,1,0:T(8,128)S(1)} %shard_map.104.heads_ref), custom_call_target="tpu_custom_call" | custom-call | flops 262144 | bytes 1048576 | tf_op jit(solution)/shard_map/pallas_call | solution.py:233
  45.6 0.9 %convert_element_type.50 = f16[32,72,128]{2,1,0:T(8,128)(2,1)} convert(f32[32,72,128]{2,1,0:T(8,128)S(1)} %shard_map.105) | non-fusion elementwise | flops 294912 | bytes 1769472 | tf_op jit(solution)/shard_map/convert_element_type | solution.py:242
  46.5 13.9 %all-to-all-start.2 = ((f16[32,72,128]{2,1,0:T(8,128)(2,1)}), f16[32,72,128]{2,1,0:T(8,128)(2,1)S(1)}, u32[]{:S(2)}, u32[]{:S(2)}) async-start(f16[32,72,128]{2,1,0:T(8,128)(2,1)} %convert_element_type.50), calls=%async_computation.2 | async-start | bytes 1179648 | tf_op jit(solution)/shard_map/all_to_all | solution.py:242
  66.9 0.6 dynamic_slice.23
  68.8 0.0 copy-done.7
  68.9 0.1 select_reduce_fusion.3
  68.9 0.6 compare_convert_fusion.extra_adds_ref
  69.6 8.1 %all-to-all-done.2 = f16[32,72,128]{2,1,0:T(8,128)(2,1)S(1)} async-done(((f16[32,72,128]{2,1,0:T(8,128)(2,1)}), f16[32,72,128]{2,1,0:T(8,128)(2,1)S(1)}, u32[]{:S(2)}, u32[]{:S(2)}) %all-to-all-start.2) | async-done | bytes 589856 | tf_op jit(solution)/shard_map/all_to_all | solution.py:242
  77.8 2.1 %shard_map.106 = (bf16[9,1792]{1,0:T(8,128)(2,1)}, f32[8,1792]{1,0:T(8,128)}, f32[8,1792]{1,0:T(8,128)}) custom-call(s32[1]{0:T(128)} %bitcast.slot_ref, s32[32]{0:T(128)S(1)} %broadcast_add_fusion.adds_ref, s32[32]{0:T(128)S(1)} %compare_convert_fusion.extra_adds_ref, f32[128,128]{1,0:T(8,128)S(1)} %broadcast_multiply_fusion.sums_ref, ...), custom_call_target="tpu_custom_call" | custom-call | flops 262144 | bytes 1048576 | tf_op jit(solution)/shard_map/pallas_call | solution.py:253
  (13 shorter events, 0.2 us)
Async XLA Ops:
  0.6 1.5 %copy-start = (bf16[1,9,57344]{2,1,0:T(8,128)(2,1)S(1)}, bf16[1,9,57344]{2,1,0:T(8,128)(2,1)}, u32[]{:S(2)}) copy-start(bf16[1,9,57344]{2,1,0:T(8,128)(2,1)} %refs_0_.1) | copy-start | bytes 3096580
  7.5 17.4 %copy-start.3 = (bf16[8,1792]{1,0:T(8,128)(2,1)S(1)}, bf16[8,1792]{1,0:T(8,128)(2,1)}, u32[]{:S(2)}) copy-start(bf16[8,1792]{1,0:T(8,128)(2,1)} %w_ref.1) | copy-start | bytes 86020
  7.5 17.5 %copy-start.1 = (f32[8,1792]{1,0:T(8,128)S(1)}, f32[8,1792]{1,0:T(8,128)}, u32[]{:S(2)}) copy-start(f32[8,1792]{1,0:T(8,128)} %s_ref.1) | copy-start | bytes 172036
  7.6 17.4 %copy-start.2 = (f32[8,1792]{1,0:T(8,128)S(1)}, f32[8,1792]{1,0:T(8,128)}, u32[]{:S(2)}) copy-start(f32[8,1792]{1,0:T(8,128)} %f_ref.1) | copy-start | bytes 172036
  7.6 21.9 %copy-start.4 = (s32[256]{0:T(256)S(1)}, s32[256]{0:T(256)}, u32[]{:S(2)}) copy-start(s32[256]{0:T(256)} %param.12) | copy-start | bytes 3076
  7.6 21.9 %copy-start.5 = (s32[256]{0:T(256)S(1)}, s32[256]{0:T(256)}, u32[]{:S(2)}) copy-start(s32[256]{0:T(256)} %param.14) | copy-start | bytes 3076
  7.6 22.0 %copy-start.6 = (s32[32]{0:T(128)S(1)}, s32[32]{0:T(128)}, u32[]{:S(2)}) copy-start(s32[32]{0:T(128)} %param.15) | copy-start | bytes 388
  8.6 35.7 %all-to-all-start.1 = ((f16[16,128,128]{2,1,0:T(8,128)(2,1)}), f16[16,128,128]{2,1,0:T(8,128)(2,1)S(1)}, u32[]{:S(2)}, u32[]{:S(2)}) async-start(f16[16,128,128]{2,1,0:T(8,128)(2,1)} %fusion.2), calls=%async_computation.1 | async-start | bytes 1048576 | tf_op jit(solution)/shard_map/all_to_all | solution.py:231
  25.0 7.3 %collective-permute-start = (f16[1,3,8,1792]{3,2,1,0:T(8,128)(2,1)S(1)}, f16[1,3,8,1792]{3,2,1,0:T(8,128)(2,1)S(1)}, u32[]{:S(2)}, u32[]{:S(2)}) collective-permute-start(f16[1,3,8,1792]{3,2,1,0:T(8,128)(2,1)S(1)} %fusion.3), channel_id=1, source_target_pairs={{0,8},{1,9},{2,10},{3,11},{4,12},{5,13},{6,14},{7,15},{8,0},{9,1},... | collective-permute-start | bytes 258056 | tf_op jit(solution)/shard_map/ppermute | solution.py:202
  32.4 8.5 %collective-permute-start.1 = (f16[2,3,8,1792]{3,2,1,0:T(8,128)(2,1)S(1)}, f16[2,3,8,1792]{3,2,1,0:T(8,128)(2,1)S(1)}, u32[]{:S(2)}, u32[]{:S(2)}) collective-permute-start(f16[2,3,8,1792]{3,2,1,0:T(8,128)(2,1)S(1)} %pad_maximum_fusion), channel_id=1, source_target_pairs={{0,4},{1,5},{2,6},{3,7},{4,0},{5,1},{6,2},{7,3},{8,12},{9,13},{10,... | collective-permute-start | bytes 516104 | tf_op jit(solution)/shard_map/ppermute | solution.py:202
  44.3 24.5 %copy-start.7 = (s32[32]{0:T(128)S(1)}, s32[32]{0:T(128)}, u32[]{:S(2)}) copy-start(s32[32]{0:T(128)} %param.13) | copy-start | bytes 388
  46.5 31.2 %all-to-all-start.2 = ((f16[32,72,128]{2,1,0:T(8,128)(2,1)}), f16[32,72,128]{2,1,0:T(8,128)(2,1)S(1)}, u32[]{:S(2)}, u32[]{:S(2)}) async-start(f16[32,72,128]{2,1,0:T(8,128)(2,1)} %convert_element_type.50), calls=%async_computation.2 | async-start | bytes 1179648 | tf_op jit(solution)/shard_map/all_to_all | solution.py:242

commit v7 on v6

--- a/solution.py
+++ b/solution.py
@@ -27,20 +27,21 @@
     return pl.CostEstimate(flops=n, bytes_accessed=4 * n, transcendentals=0)
 
 
-def split_kernel(homes, width, steps, grads_ref, out_ref, line):
+def split_kernel(homes, width, steps, grads_ref, keep_ref, send_ref, line):
     tiles = width // LANES
     line[...] = jnp.zeros_like(line)
+    core = lax.axis_index("core")
     for j in range(steps):
-        for c in range(2):
-            at = (2 * j + c) * width
-            block = grads_ref[0, :, at : at + width].astype(F32)
+        for c, out_ref in ((core, keep_ref), (1 - core, send_ref)):
+            at = pl.multiple_of((2 * j + c) * width, LANES)
+            block = grads_ref[0, :, pl.ds(at, width)].astype(F32)
             for t in range(0, tiles, 2):
                 low = block[:homes, t * LANES : (t + 1) * LANES]
                 high = block[:homes, (t + 1) * LANES : (t + 2) * LANES]
-                out_ref[c, j, t * homes : (t + 2) * homes, :] = jnp.concatenate([low, high], axis=0).astype(BF16)
+                out_ref[j, t * homes : (t + 2) * homes, :] = jnp.concatenate([low, high], axis=0).astype(BF16)
             for t in range(tiles):
                 line[t : t + 1, :] = block[homes : homes + 1, t * LANES : (t + 1) * LANES]
-            out_ref[c, j, tiles * homes : tiles * homes + ROW, :] = line[...].astype(BF16)
+            out_ref[j, tiles * homes : tiles * homes + ROW, :] = line[...].astype(BF16)
 
 
 def split_by_core(grads, outer, width):
@@ -51,8 +52,8 @@
         lambda *refs: split_kernel(homes, width, steps, *refs),
         grid=(outer // steps,),
         in_specs=[pl.BlockSpec((1, homes + 1, steps * 2 * width), lambda i: (0, 0, i))],
-        out_specs=pl.BlockSpec((2, steps, rows, LANES), lambda i: (0, i, 0, 0)),
-        out_shape=jax.ShapeDtypeStruct((2, outer, rows, LANES), BF16),
+        out_specs=[pl.BlockSpec((steps, rows, LANES), lambda i: (i, 0, 0))] * 2,
+        out_shape=[jax.ShapeDtypeStruct((outer, rows, LANES), BF16)] * 2,
         scratch_shapes=[pltpu.VMEM((ROW, LANES), F32)],
         compiler_params=pltpu.CompilerParams(vmem_limit_bytes=16 * 2**20),
         cost_estimate=cost(1 << 19),
@@ -225,9 +226,9 @@
         compiler_params=pltpu.CompilerParams(vmem_limit_bytes=16 * 2**20),
         cost_estimate=cost(1 << 18),
     )(mine, moves, wants, held)
-    halves = split_by_core(grads, outer, width)
-    pair = lax.all_to_all(halves, "core", 0, 0, tiled=True).astype(F32)
-    partial = ((pair[0] + pair[1]) * PAIR_SCALE).astype(F16)
+    kept, sent = split_by_core(grads, outer, width)
+    other = lax.ppermute(sent, "core", [(0, 1), (1, 0)])
+    partial = ((kept.astype(F32) + other.astype(F32)) * PAIR_SCALE).astype(F16)
     parts = lax.all_to_all(partial, "outer", 0, 0, tiled=True)
     sums = jnp.sum(parts.astype(F32), axis=0) * (1.0 / PAIR_SCALE)
     outgoing = pl.pallas_call(

time: 80.5 us -> 83.2 us (1.034)
  waiting for transfers between devices: 14.9 us -> 19.8 us
  blocking collectives: 4.58 us -> 0 us
  starting transfers between devices: 39.4 us -> 42 us
    all_to_all x1, waiting for transfers between devices: 2.51 us -> 7.36 us  [per_device(): parts = lax.all_to_all(partial, 'outer', 0, 0, tiled=True)]
    all_to_all x1 -> x0, blocking collectives: 4.58 us -> none  [per_device(): pair = lax.all_to_all(halves, 'core', 0, 0, tiled=True).astype(F32)]
    ppermute x2, starting transfers between devices: 9.07 us -> 13.1 us  [share_states(): other = lax.ppermute(held, 'expert', [(i, i ^ bit) for i in range(devices)])]
    all_to_all x1, starting transfers between devices: 16.4 us -> 12.9 us  [per_device(): parts = lax.all_to_all(partial, 'outer', 0, 0, tiled=True)]
    ppermute x0 -> x1, starting transfers between devices: none -> 1.92 us  [per_device(): other = lax.ppermute(sent, 'core', [(0, 1), (1, 0)])]
  transfers between devices with their start and end apart: 4 -> 5, of which waited for: 4 -> 3; matrix products, arithmetic and copies ran while one was open for 5% -> 6% of each run, Pallas kernels for 1% -> 1%
where the time goes in v7:
time: 83.2 us; the launch traced here: 82.6 us
  starting transfers between devices  42 us (50%)
  waiting for transfers between devices  19.8 us (24%)
  between operations  8.76 us (11%)
  other arithmetic  5.2 us (6%)
  Pallas kernels  4.74 us (6%)
  local copies, waits for them, and re-layouts  2.14 us (3%)
    all_to_all x1, starting transfers between devices, per_device(): arrived = lax.all_to_all(outgoing.astype(F16), 'expert', 0, 0, tiled=True)  14.2 us
    ppermute x2, starting transfers between devices, share_states(): other = lax.ppermute(held, 'expert', [(i, i ^ bit) for i in range(devices)])  13.1 us
    all_to_all x1, starting transfers between devices, per_device(): parts = lax.all_to_all(partial, 'outer', 0, 0, tiled=True)  12.9 us
    all_to_all x1, waiting for transfers between devices, per_device(): arrived = lax.all_to_all(outgoing.astype(F16), 'expert', 0, 0, tiled=True)  8.24 us
    all_to_all x1, waiting for transfers between devices, per_device(): parts = lax.all_to_all(partial, 'outer', 0, 0, tiled=True)  7.36 us
    ppermute x2, waiting for transfers between devices, share_states(): other = lax.ppermute(held, 'expert', [(i, i ^ bit) for i in range(devices)])  4.16 us
    pallas_call x1, Pallas kernels, per_device(): pl.pallas_call(final_kernel, in_specs=[SMEM] * 3 + [VMEM] * 7, out_specs=...  2.14 us
    ppermute x1, starting transfers between devices, per_device(): other = lax.ppermute(sent, 'core', [(0, 1), (1, 0)])  1.92 us
  transfers between devices with their start and end apart: 5, of which 3 were waited for; matrix products, arithmetic and copies ran while one was open for 6% of the time, Pallas kernels for 1%

profile of v7, /device:TPU:14, one launch (start us, length us, event | category | flops | bytes accessed | tf_op | source)
XLA Modules:
  0.0 82.6 jit_solution(1374758456396650577)
XLA Ops:
  0.6 0.0 copy-start
  0.6 1.5 %copy-done = bf16[1,9,57344]{2,1,0:T(8,128)(2,1)S(1)} copy-done((bf16[1,9,57344]{2,1,0:T(8,128)(2,1)S(1)}, bf16[1,9,57344]{2,1,0:T(8,128)(2,1)}, u32[]{:S(2)}) %copy-start) | copy-done | bytes 1032216
  2.1 0.0 copy-start.3
  2.1 0.0 copy-start.1
  2.1 0.0 copy-start.2
  2.1 0.0 copy-start.4
  2.1 0.0 copy-start.5
  2.2 0.0 copy-start.6
  2.2 0.5 shard_map.103
  2.7 1.9 %collective-permute-start = (bf16[16,128,128]{2,1,0:T(8,128)(2,1)S(1)}, bf16[16,128,128]{2,1,0:T(8,128)(2,1)S(1)}, u32[]{:S(2)}, u32[]{:S(2)}) collective-permute-start(bf16[16,128,128]{2,1,0:T(8,128)(2,1)S(1)} %get-tuple-element.6), channel_id=1, source_target_pairs={{0,32},{32,0},{1,33},{33,1},{2,34},{34,2},{3,35},{35,3},{4,36},{36... | collective-permute-start | bytes 1572872 | tf_op jit(solution)/shard_map/ppermute | solution.py:230
  4.6 0.0 copy-done.3
  4.7 0.0 copy-done.1
  4.7 0.0 copy-done.2
  4.7 7.9 %collective-permute-start.1 = (f16[1,3,8,1792]{3,2,1,0:T(8,128)(2,1)S(1)}, f16[1,3,8,1792]{3,2,1,0:T(8,128)(2,1)S(1)}, u32[]{:S(2)}, u32[]{:S(2)}) collective-permute-start(f16[1,3,8,1792]{3,2,1,0:T(8,128)(2,1)S(1)} %fusion), channel_id=1, source_target_pairs={{0,8},{1,9},{2,10},{3,11},{4,12},{5,13},{6,14},{7,15},{8,0},{9,1},... | collective-permute-start | bytes 258056 | tf_op jit(solution)/shard_map/ppermute | solution.py:203
  12.7 0.0 copy-done.4
  12.7 0.0 copy-done.5
  12.7 0.1 select_reduce_fusion.1
  12.8 0.0 copy-done.6
  12.8 0.2 select_reduce_fusion
  13.0 0.6 fusion.5
  13.7 0.0 collective-permute-done
  13.7 1.0 %multiply_convert_fusion = f16[16,128,128]{2,1,0:T(8,128)(2,1)} fusion(bf16[16,128,128]{2,1,0:T(8,128)(2,1)S(1)} %collective-permute-done, bf16[16,128,128]{2,1,0:T(8,128)(2,1)S(1)} %get-tuple-element.5), kind=kLoop, calls=%fused_computation.1 | loop fusion | flops 1310720 | bytes 1572864 | tf_op jit(solution)/shard_map/convert_element_type | solution.py:231
  14.7 12.9 %all-to-all-start = ((f16[16,128,128]{2,1,0:T(8,128)(2,1)}), f16[16,128,128]{2,1,0:T(8,128)(2,1)S(1)}, u32[]{:S(2)}, u32[]{:S(2)}) async-start(f16[16,128,128]{2,1,0:T(8,128)(2,1)} %multiply_convert_fusion), calls=%async_computation | async-start | bytes 1048576 | tf_op jit(solution)/shard_map/all_to_all | solution.py:232
  27.5 0.6 fusion.4
  28.2 0.7 fusion.6
  28.9 0.0 collective-permute-done.1
  28.9 5.2 %collective-permute-start.2 = (f16[2,3,8,1792]{3,2,1,0:T(8,128)(2,1)S(1)}, f16[2,3,8,1792]{3,2,1,0:T(8,128)(2,1)S(1)}, u32[]{:S(2)}, u32[]{:S(2)}) collective-permute-start(f16[2,3,8,1792]{3,2,1,0:T(8,128)(2,1)S(1)} %pad_maximum_fusion), channel_id=1, source_target_pairs={{0,4},{1,5},{2,6},{3,7},{4,0},{5,1},{6,2},{7,3},{8,12},{9,13},{10,... | collective-permute-start | bytes 516104 | tf_op jit(solution)/shard_map/ppermute | solution.py:203
  34.1 4.2 %collective-permute-done.2 = f16[2,3,8,1792]{3,2,1,0:T(8,128)(2,1)S(1)} collective-permute-done((f16[2,3,8,1792]{3,2,1,0:T(8,128)(2,1)S(1)}, f16[2,3,8,1792]{3,2,1,0:T(8,128)(2,1)S(1)}, u32[]{:S(2)}, u32[]{:S(2)}) %collective-permute-start.2) | collective-permute-done | bytes 172064 | tf_op jit(solution)/shard_map/ppermute | solution.py:203
  38.3 0.1 maximum_convert_fusion.held_ref
  38.4 0.8 %shard_map.104.heads_ref = f32[32,24,128]{2,1,0:T(8,128)S(1)} custom-call(s32[1]{0:T(128)} %bitcast.2.mine_ref, s32[32]{0:T(128)S(1)} %get-tuple-element.22.moves_ref, s32[32]{0:T(128)S(1)} %get-tuple-element.20.wants_ref, f32[4,3,8,1792]{3,2,1,0:T(8,128)S(1)} %maximum_convert_fusion.held_ref), custom_call_target="tpu_custom_call" | custom-call | flops 262144 | bytes 1048576 | tf_op jit(solution)/shard_map/pallas_call | solution.py:220
  39.2 7.4 %all-to-all-done = f16[16,128,128]{2,1,0:T(8,128)(2,1)S(1)} async-done(((f16[16,128,128]{2,1,0:T(8,128)(2,1)}), f16[16,128,128]{2,1,0:T(8,128)(2,1)S(1)}, u32[]{:S(2)}, u32[]{:S(2)}) %all-to-all-start) | async-done | bytes 524320 | tf_op jit(solution)/shard_map/all_to_all | solution.py:232
  46.6 0.1 convert_reduce_fusion
  46.7 1.2 %shard_map.105 = f32[32,72,128]{2,1,0:T(8,128)S(1)} custom-call(s32[1]{0:T(128)} %bitcast.slot_ref, s32[32]{0:T(128)S(1)} %get-tuple-element.21.asked_ref, f32[128,128]{1,0:T(8,128)S(1)} %broadcast_multiply_fusion.sums_ref, f32[32,24,128]{2,1,0:T(8,128)S(1)} %shard_map.104.heads_ref), custom_call_target="tpu_custom_call" | custom-call | flops 262144 | bytes 1048576 | tf_op jit(solution)/shard_map/pallas_call | solution.py:234
  47.9 0.0 copy-start.7
  47.9 0.9 %convert_element_type.50 = f16[32,72,128]{2,1,0:T(8,128)(2,1)} convert(f32[32,72,128]{2,1,0:T(8,128)S(1)} %shard_map.105) | non-fusion elementwise | flops 294912 | bytes 1769472 | tf_op jit(solution)/shard_map/convert_element_type | solution.py:243
  48.8 14.2 %all-to-all-start.1 = ((f16[32,72,128]{2,1,0:T(8,128)(2,1)}), f16[32,72,128]{2,1,0:T(8,128)(2,1)S(1)}, u32[]{:S(2)}, u32[]{:S(2)}) async-start(f16[32,72,128]{2,1,0:T(8,128)(2,1)} %convert_element_type.50), calls=%async_computation.1 | async-start | bytes 1179648 | tf_op jit(solution)/shard_map/all_to_all | solution.py:243
  69.5 0.6 dynamic_slice.23
  71.4 0.0 copy-done.7
  71.4 0.1 select_reduce_fusion.3
  71.5 0.6 compare_convert_fusion.extra_adds_ref
  72.1 8.2 %all-to-all-done.1 = f16[32,72,128]{2,1,0:T(8,128)(2,1)S(1)} async-done(((f16[32,72,128]{2,1,0:T(8,128)(2,1)}), f16[32,72,128]{2,1,0:T(8,128)(2,1)S(1)}, u32[]{:S(2)}, u32[]{:S(2)}) %all-to-all-start.1) | async-done | bytes 589856 | tf_op jit(solution)/shard_map/all_to_all | solution.py:243
  80.5 2.1 %shard_map.106 = (bf16[9,1792]{1,0:T(8,128)(2,1)}, f32[8,1792]{1,0:T(8,128)}, f32[8,1792]{1,0:T(8,128)}) custom-call(s32[1]{0:T(128)} %bitcast.slot_ref, s32[32]{0:T(128)S(1)} %broadcast_add_fusion.adds_ref, s32[32]{0:T(128)S(1)} %compare_convert_fusion.extra_adds_ref, f32[128,128]{1,0:T(8,128)S(1)} %broadcast_multiply_fusion.sums_ref, ...), custom_call_target="tpu_custom_call" | custom-call | flops 262144 | bytes 1048576 | tf_op jit(solution)/shard_map/pallas_call | solution.py:254
  (13 shorter events, 0.2 us)
Async XLA Ops:
  0.6 1.5 %copy-start = (bf16[1,9,57344]{2,1,0:T(8,128)(2,1)S(1)}, bf16[1,9,57344]{2,1,0:T(8,128)(2,1)}, u32[]{:S(2)}) copy-start(bf16[1,9,57344]{2,1,0:T(8,128)(2,1)} %refs_0_.1) | copy-start | bytes 3096580
  2.1 2.5 %copy-start.3 = (bf16[8,1792]{1,0:T(8,128)(2,1)S(1)}, bf16[8,1792]{1,0:T(8,128)(2,1)}, u32[]{:S(2)}) copy-start(bf16[8,1792]{1,0:T(8,128)(2,1)} %w_ref.1) | copy-start | bytes 86020
  2.1 2.5 %copy-start.1 = (f32[8,1792]{1,0:T(8,128)S(1)}, f32[8,1792]{1,0:T(8,128)}, u32[]{:S(2)}) copy-start(f32[8,1792]{1,0:T(8,128)} %s_ref.1) | copy-start | bytes 172036
  2.1 2.5 %copy-start.2 = (f32[8,1792]{1,0:T(8,128)S(1)}, f32[8,1792]{1,0:T(8,128)}, u32[]{:S(2)}) copy-start(f32[8,1792]{1,0:T(8,128)} %f_ref.1) | copy-start | bytes 172036
  2.1 10.5 %copy-start.4 = (s32[256]{0:T(256)S(1)}, s32[256]{0:T(256)}, u32[]{:S(2)}) copy-start(s32[256]{0:T(256)} %param.12) | copy-start | bytes 3076
  2.1 10.5 %copy-start.5 = (s32[256]{0:T(256)S(1)}, s32[256]{0:T(256)}, u32[]{:S(2)}) copy-start(s32[256]{0:T(256)} %param.14) | copy-start | bytes 3076
  2.2 10.7 %copy-start.6 = (s32[32]{0:T(128)S(1)}, s32[32]{0:T(128)}, u32[]{:S(2)}) copy-start(s32[32]{0:T(128)} %param.15) | copy-start | bytes 388
  2.7 11.0 %collective-permute-start = (bf16[16,128,128]{2,1,0:T(8,128)(2,1)S(1)}, bf16[16,128,128]{2,1,0:T(8,128)(2,1)S(1)}, u32[]{:S(2)}, u32[]{:S(2)}) collective-permute-start(bf16[16,128,128]{2,1,0:T(8,128)(2,1)S(1)} %get-tuple-element.6), channel_id=1, source_target_pairs={{0,32},{32,0},{1,33},{33,1},{2,34},{34,2},{3,35},{35,3},{4,36},{36... | collective-permute-start | bytes 1572872 | tf_op jit(solution)/shard_map/ppermute | solution.py:230
  4.7 24.1 %collective-permute-start.1 = (f16[1,3,8,1792]{3,2,1,0:T(8,128)(2,1)S(1)}, f16[1,3,8,1792]{3,2,1,0:T(8,128)(2,1)S(1)}, u32[]{:S(2)}, u32[]{:S(2)}) collective-permute-start(f16[1,3,8,1792]{3,2,1,0:T(8,128)(2,1)S(1)} %fusion), channel_id=1, source_target_pairs={{0,8},{1,9},{2,10},{3,11},{4,12},{5,13},{6,14},{7,15},{8,0},{9,1},... | collective-permute-start | bytes 258056 | tf_op jit(solution)/shard_map/ppermute | solution.py:203
  14.7 31.9 %all-to-all-start = ((f16[16,128,128]{2,1,0:T(8,128)(2,1)}), f16[16,128,128]{2,1,0:T(8,128)(2,1)S(1)}, u32[]{:S(2)}, u32[]{:S(2)}) async-start(f16[16,128,128]{2,1,0:T(8,128)(2,1)} %multiply_convert_fusion), calls=%async_computation | async-start | bytes 1048576 | tf_op jit(solution)/shard_map/all_to_all | solution.py:232
  28.9 9.4 %collective-permute-start.2 = (f16[2,3,8,1792]{3,2,1,0:T(8,128)(2,1)S(1)}, f16[2,3,8,1792]{3,2,1,0:T(8,128)(2,1)S(1)}, u32[]{:S(2)}, u32[]{:S(2)}) collective-permute-start(f16[2,3,8,1792]{3,2,1,0:T(8,128)(2,1)S(1)} %pad_maximum_fusion), channel_id=1, source_target_pairs={{0,4},{1,5},{2,6},{3,7},{4,0},{5,1},{6,2},{7,3},{8,12},{9,13},{10,... | collective-permute-start | bytes 516104 | tf_op jit(solution)/shard_map/ppermute | solution.py:203
  47.9 23.5 %copy-start.7 = (s32[32]{0:T(128)S(1)}, s32[32]{0:T(128)}, u32[]{:S(2)}) copy-start(s32[32]{0:T(128)} %param.13) | copy-start | bytes 388
  48.8 31.6 %all-to-all-start.1 = ((f16[32,72,128]{2,1,0:T(8,128)(2,1)}), f16[32,72,128]{2,1,0:T(8,128)(2,1)S(1)}, u32[]{:S(2)}, u32[]{:S(2)}) async-start(f16[32,72,128]{2,1,0:T(8,128)(2,1)} %convert_element_type.50), calls=%async_computation.1 | async-start | bytes 1179648 | tf_op jit(solution)/shard_map/all_to_all | solution.py:243

commit v8 on v6

--- a/solution.py
+++ b/solution.py
@@ -54,7 +54,6 @@
         out_specs=pl.BlockSpec((2, steps, rows, LANES), lambda i: (0, i, 0, 0)),
         out_shape=jax.ShapeDtypeStruct((2, outer, rows, LANES), BF16),
         scratch_shapes=[pltpu.VMEM((ROW, LANES), F32)],
-        compiler_params=pltpu.CompilerParams(vmem_limit_bytes=16 * 2**20),
         cost_estimate=cost(1 << 19),
     )(grads)
 

time: 80.5 us -> 83.3 us (1.035)
  Pallas kernels: 4.79 us -> 7.88 us
  local copies, waits for them, and re-layouts: 2.16 us -> 0.66 us
  blocking collectives: 4.58 us -> 5.68 us
    pallas_call x1, Pallas kernels: 0.58 us -> 3.67 us  [split_by_core(): pl.pallas_call(lambda *refs: split_kernel(homes, width, steps, *refs), gr...]
    unnamed x16 -> x14, local copies, waits for them, and re-layouts: 1.54 us -> 0.04 us
    all_to_all x1, blocking collectives: 4.58 us -> 5.68 us  [per_device(): pair = lax.all_to_all(halves, 'core', 0, 0, tiled=True).astype(F32)]
where the time goes in v8:
time: 83.3 us; the launch traced here: 82.6 us
  starting transfers between devices  39.4 us (47%)
  waiting for transfers between devices  14.9 us (18%)
  between operations  8.76 us (11%)
  Pallas kernels  7.88 us (9%)
  blocking collectives  5.68 us (7%)
  other arithmetic  5.39 us (6%)
    all_to_all x1, starting transfers between devices, per_device(): parts = lax.all_to_all(partial, 'outer', 0, 0, tiled=True)  16.4 us
    all_to_all x1, starting transfers between devices, per_device(): arrived = lax.all_to_all(outgoing.astype(F16), 'expert', 0, 0, tiled=True)  13.9 us
    ppermute x2, starting transfers between devices, share_states(): other = lax.ppermute(held, 'expert', [(i, i ^ bit) for i in range(devices)])  9.07 us
    all_to_all x1, waiting for transfers between devices, per_device(): arrived = lax.all_to_all(outgoing.astype(F16), 'expert', 0, 0, tiled=True)  8.09 us
    all_to_all x1, blocking collectives, per_device(): pair = lax.all_to_all(halves, 'core', 0, 0, tiled=True).astype(F32)  5.68 us
    ppermute x2, waiting for transfers between devices, share_states(): other = lax.ppermute(held, 'expert', [(i, i ^ bit) for i in range(devices)])  4.27 us
    pallas_call x1, Pallas kernels, split_by_core(): pl.pallas_call(lambda *refs: split_kernel(homes, width, steps, *refs), gr...  3.67 us
    all_to_all x1, waiting for transfers between devices, per_device(): parts = lax.all_to_all(partial, 'outer', 0, 0, tiled=True)  2.5 us
  transfers between devices with their start and end apart: 4, of which 4 were waited for; matrix products, arithmetic and copies ran while one was open for 5% of the time, Pallas kernels for 1%

profile of v8, /device:TPU:14, one launch (start us, length us, event | category | flops | bytes accessed | tf_op | source)
XLA Modules:
  0.0 82.6 jit_solution(10643065152907258078)
XLA Ops:
  0.6 3.7 %shard_map.103 = bf16[2,16,128,128]{3,2,1,0:T(8,128)(2,1)} custom-call(bf16[1,9,57344]{2,1,0:T(8,128)(2,1)} %refs_0_.1), custom_call_target="tpu_custom_call" | custom-call | flops 524288 | bytes 2097152 | tf_op jit(solution)/shard_map/pallas_call | solution.py:50
  4.3 5.7 %all_to_all.15 = bf16[2,16,128,128]{3,2,1,0:T(8,128)(2,1)S(1)} all-to-all(bf16[2,16,128,128]{3,2,1,0:T(8,128)(2,1)} %shard_map.103), channel_id=1, replica_groups=mesh['outer'=16,'core'=2,'expert'=32] {'core'}, dimensions={0} | all-to-all | bytes 2097152 | tf_op jit(solution)/shard_map/all_to_all | solution.py:228
  10.0 0.2 convert_element_type.44
  10.2 0.0 copy-start.2
  10.2 0.0 copy-start
  10.2 0.0 copy-start.1
  10.3 0.0 copy-start.3
  10.3 0.0 copy-start.4
  10.3 0.0 copy-start.5
  10.3 1.0 %fusion.2 = f16[16,128,128]{2,1,0:T(8,128)(2,1)} fusion(f32[2,16,128,128]{3,2,1,0:T(8,128)S(1)} %convert_element_type.44), kind=kLoop, calls=%fused_computation.4 | loop fusion | flops 786432 | bytes 2621440 | tf_op jit(solution)/shard_map/convert_element_type | solution.py:229
  11.2 16.4 %all-to-all-start.1 = ((f16[16,128,128]{2,1,0:T(8,128)(2,1)}), f16[16,128,128]{2,1,0:T(8,128)(2,1)S(1)}, u32[]{:S(2)}, u32[]{:S(2)}) async-start(f16[16,128,128]{2,1,0:T(8,128)(2,1)} %fusion.2), calls=%async_computation.1 | async-start | bytes 1048576 | tf_op jit(solution)/shard_map/all_to_all | solution.py:230
  27.7 0.0 copy-done.2
  27.7 0.0 copy-done
  27.7 0.0 copy-done.1
  27.7 4.3 %collective-permute-start = (f16[1,3,8,1792]{3,2,1,0:T(8,128)(2,1)S(1)}, f16[1,3,8,1792]{3,2,1,0:T(8,128)(2,1)S(1)}, u32[]{:S(2)}, u32[]{:S(2)}) collective-permute-start(f16[1,3,8,1792]{3,2,1,0:T(8,128)(2,1)S(1)} %fusion.3), channel_id=1, source_target_pairs={{0,8},{1,9},{2,10},{3,11},{4,12},{5,13},{6,14},{7,15},{8,0},{9,1},... | collective-permute-start | bytes 258056 | tf_op jit(solution)/shard_map/ppermute | solution.py:201
  32.1 0.0 copy-done.3
  32.1 0.0 copy-done.4
  32.2 0.1 select_reduce_fusion.1
  32.3 0.0 copy-done.5
  32.3 0.2 select_reduce_fusion
  32.5 0.6 fusion.8
  33.1 0.6 fusion.7
  33.7 0.7 fusion.9
  34.4 0.6 collective-permute-done
  35.1 4.7 %collective-permute-start.1 = (f16[2,3,8,1792]{3,2,1,0:T(8,128)(2,1)S(1)}, f16[2,3,8,1792]{3,2,1,0:T(8,128)(2,1)S(1)}, u32[]{:S(2)}, u32[]{:S(2)}) collective-permute-start(f16[2,3,8,1792]{3,2,1,0:T(8,128)(2,1)S(1)} %pad_maximum_fusion), channel_id=1, source_target_pairs={{0,4},{1,5},{2,6},{3,7},{4,0},{5,1},{6,2},{7,3},{8,12},{9,13},{10,... | collective-permute-start | bytes 516104 | tf_op jit(solution)/shard_map/ppermute | solution.py:201
  39.8 3.7 %collective-permute-done.1 = f16[2,3,8,1792]{3,2,1,0:T(8,128)(2,1)S(1)} collective-permute-done((f16[2,3,8,1792]{3,2,1,0:T(8,128)(2,1)S(1)}, f16[2,3,8,1792]{3,2,1,0:T(8,128)(2,1)S(1)}, u32[]{:S(2)}, u32[]{:S(2)}) %collective-permute-start.1) | collective-permute-done | bytes 172064 | tf_op jit(solution)/shard_map/ppermute | solution.py:201
  43.5 0.1 maximum_convert_fusion.held_ref
  43.6 0.8 %shard_map.104.heads_ref = f32[32,24,128]{2,1,0:T(8,128)S(1)} custom-call(s32[1]{0:T(128)} %bitcast.3.mine_ref, s32[32]{0:T(128)S(1)} %get-tuple-element.18.moves_ref, s32[32]{0:T(128)S(1)} %get-tuple-element.16.wants_ref, f32[4,3,8,1792]{3,2,1,0:T(8,128)S(1)} %maximum_convert_fusion.held_ref), custom_call_target="tpu_custom_call" | custom-call | flops 262144 | bytes 1048576 | tf_op jit(solution)/shard_map/pallas_call | solution.py:218
  44.4 2.5 %all-to-all-done.1 = f16[16,128,128]{2,1,0:T(8,128)(2,1)S(1)} async-done(((f16[16,128,128]{2,1,0:T(8,128)(2,1)}), f16[16,128,128]{2,1,0:T(8,128)(2,1)S(1)}, u32[]{:S(2)}, u32[]{:S(2)}) %all-to-all-start.1) | async-done | bytes 524320 | tf_op jit(solution)/shard_map/all_to_all | solution.py:230
  46.9 0.1 convert_reduce_fusion
  47.0 0.0 copy-start.6
  47.0 1.2 %shard_map.105 = f32[32,72,128]{2,1,0:T(8,128)S(1)} custom-call(s32[1]{0:T(128)} %bitcast.slot_ref, s32[32]{0:T(128)S(1)} %get-tuple-element.17.asked_ref, f32[128,128]{1,0:T(8,128)S(1)} %broadcast_multiply_fusion.sums_ref, f32[32,24,128]{2,1,0:T(8,128)S(1)} %shard_map.104.heads_ref), custom_call_target="tpu_custom_call" | custom-call | flops 262144 | bytes 1048576 | tf_op jit(solution)/shard_map/pallas_call | solution.py:232
  48.3 0.9 %convert_element_type.50 = f16[32,72,128]{2,1,0:T(8,128)(2,1)} convert(f32[32,72,128]{2,1,0:T(8,128)S(1)} %shard_map.105) | non-fusion elementwise | flops 294912 | bytes 1769472 | tf_op jit(solution)/shard_map/convert_element_type | solution.py:241
  49.2 13.9 %all-to-all-start.2 = ((f16[32,72,128]{2,1,0:T(8,128)(2,1)}), f16[32,72,128]{2,1,0:T(8,128)(2,1)S(1)}, u32[]{:S(2)}, u32[]{:S(2)}) async-start(f16[32,72,128]{2,1,0:T(8,128)(2,1)} %convert_element_type.50), calls=%async_computation.2 | async-start | bytes 1179648 | tf_op jit(solution)/shard_map/all_to_all | solution.py:241
  69.6 0.6 dynamic_slice.23
  71.5 0.0 copy-done.6
  71.5 0.1 select_reduce_fusion.3
  71.6 0.6 compare_convert_fusion.extra_adds_ref
  72.3 8.1 %all-to-all-done.2 = f16[32,72,128]{2,1,0:T(8,128)(2,1)S(1)} async-done(((f16[32,72,128]{2,1,0:T(8,128)(2,1)}), f16[32,72,128]{2,1,0:T(8,128)(2,1)S(1)}, u32[]{:S(2)}, u32[]{:S(2)}) %all-to-all-start.2) | async-done | bytes 589856 | tf_op jit(solution)/shard_map/all_to_all | solution.py:241
  80.5 2.1 %shard_map.106 = (bf16[9,1792]{1,0:T(8,128)(2,1)}, f32[8,1792]{1,0:T(8,128)}, f32[8,1792]{1,0:T(8,128)}) custom-call(s32[1]{0:T(128)} %bitcast.slot_ref, s32[32]{0:T(128)S(1)} %broadcast_add_fusion.adds_ref, s32[32]{0:T(128)S(1)} %compare_convert_fusion.extra_adds_ref, f32[128,128]{1,0:T(8,128)S(1)} %broadcast_multiply_fusion.sums_ref, ...), custom_call_target="tpu_custom_call" | custom-call | flops 262144 | bytes 1048576 | tf_op jit(solution)/shard_map/pallas_call | solution.py:252
  (13 shorter events, 0.2 us)
Async XLA Ops:
  10.2 17.4 %copy-start.2 = (bf16[8,1792]{1,0:T(8,128)(2,1)S(1)}, bf16[8,1792]{1,0:T(8,128)(2,1)}, u32[]{:S(2)}) copy-start(bf16[8,1792]{1,0:T(8,128)(2,1)} %w_ref.1) | copy-start | bytes 86020
  10.2 17.5 %copy-start = (f32[8,1792]{1,0:T(8,128)S(1)}, f32[8,1792]{1,0:T(8,128)}, u32[]{:S(2)}) copy-start(f32[8,1792]{1,0:T(8,128)} %s_ref.1) | copy-start | bytes 172036
  10.2 17.4 %copy-start.1 = (f32[8,1792]{1,0:T(8,128)S(1)}, f32[8,1792]{1,0:T(8,128)}, u32[]{:S(2)}) copy-start(f32[8,1792]{1,0:T(8,128)} %f_ref.1) | copy-start | bytes 172036
  10.3 21.9 %copy-start.3 = (s32[256]{0:T(256)S(1)}, s32[256]{0:T(256)}, u32[]{:S(2)}) copy-start(s32[256]{0:T(256)} %param.12) | copy-start | bytes 3076
  10.3 21.9 %copy-start.4 = (s32[256]{0:T(256)S(1)}, s32[256]{0:T(256)}, u32[]{:S(2)}) copy-start(s32[256]{0:T(256)} %param.14) | copy-start | bytes 3076
  10.3 22.0 %copy-start.5 = (s32[32]{0:T(128)S(1)}, s32[32]{0:T(128)}, u32[]{:S(2)}) copy-start(s32[32]{0:T(128)} %param.15) | copy-start | bytes 388
  11.2 35.7 %all-to-all-start.1 = ((f16[16,128,128]{2,1,0:T(8,128)(2,1)}), f16[16,128,128]{2,1,0:T(8,128)(2,1)S(1)}, u32[]{:S(2)}, u32[]{:S(2)}) async-start(f16[16,128,128]{2,1,0:T(8,128)(2,1)} %fusion.2), calls=%async_computation.1 | async-start | bytes 1048576 | tf_op jit(solution)/shard_map/all_to_all | solution.py:230
  27.7 7.3 %collective-permute-start = (f16[1,3,8,1792]{3,2,1,0:T(8,128)(2,1)S(1)}, f16[1,3,8,1792]{3,2,1,0:T(8,128)(2,1)S(1)}, u32[]{:S(2)}, u32[]{:S(2)}) collective-permute-start(f16[1,3,8,1792]{3,2,1,0:T(8,128)(2,1)S(1)} %fusion.3), channel_id=1, source_target_pairs={{0,8},{1,9},{2,10},{3,11},{4,12},{5,13},{6,14},{7,15},{8,0},{9,1},... | collective-permute-start | bytes 258056 | tf_op jit(solution)/shard_map/ppermute | solution.py:201
  35.1 8.5 %collective-permute-start.1 = (f16[2,3,8,1792]{3,2,1,0:T(8,128)(2,1)S(1)}, f16[2,3,8,1792]{3,2,1,0:T(8,128)(2,1)S(1)}, u32[]{:S(2)}, u32[]{:S(2)}) collective-permute-start(f16[2,3,8,1792]{3,2,1,0:T(8,128)(2,1)S(1)} %pad_maximum_fusion), channel_id=1, source_target_pairs={{0,4},{1,5},{2,6},{3,7},{4,0},{5,1},{6,2},{7,3},{8,12},{9,13},{10,... | collective-permute-start | bytes 516104 | tf_op jit(solution)/shard_map/ppermute | solution.py:201
  47.0 24.5 %copy-start.6 = (s32[32]{0:T(128)S(1)}, s32[32]{0:T(128)}, u32[]{:S(2)}) copy-start(s32[32]{0:T(128)} %param.13) | copy-start | bytes 388
  49.2 31.2 %all-to-all-start.2 = ((f16[32,72,128]{2,1,0:T(8,128)(2,1)}), f16[32,72,128]{2,1,0:T(8,128)(2,1)S(1)}, u32[]{:S(2)}, u32[]{:S(2)}) async-start(f16[32,72,128]{2,1,0:T(8,128)(2,1)} %convert_element_type.50), calls=%async_computation.2 | async-start | bytes 1179648 | tf_op jit(solution)/shard_map/all_to_all | solution.py:241
